TPU v7x, 32 devices: a whole 2x2x4 slice. The times are simulated.
32 devices in a mesh: expert: 8 (over y, x, core), replica: 4 (over z).
Axes of the slice: x: 2, y: 2, z: 4, core: 2. Of those that a mesh axis runs over, the one named last changes fastest.
Arguments:
- x_rows: bfloat16 [4096, 2048], P(('expert', 'replica')), may hold values from -6 to 6
- out_grad: bfloat16 [4096, 2048], P(('expert', 'replica')), may hold values from -6 to 6
- gate_weight: bfloat16 [16, 2048, 768], P('expert', 'replica'), may hold values from -0.125 to 0.125
- up_weight: bfloat16 [16, 2048, 768], P('expert', 'replica'), may hold values from -0.125 to 0.125
- down_weight: bfloat16 [16, 2048, 768], P('expert', 'replica'), may hold values from -0.21875 to 0.21875
- expert_ids: int32 [4096], P(('expert', 'replica')), may hold values from 0 to 15, as said below
- slot_expert: int32 [8, 4], replicated, may hold values from 0 to 15, as said below
Outputs:
- x_grad: bfloat16 [4096, 2048], P(('expert', 'replica'))
- gate_wgrad: bfloat16 [16, 2048, 768], P('expert', 'replica')
- up_wgrad: bfloat16 [16, 2048, 768], P('expert', 'replica')
- down_wgrad: bfloat16 [16, 2048, 768], P('expert', 'replica')
Inputs may be any that keep to these rules, and one draw needn't show every extreme that they name: `expert_ids`: each device's 128 rows name each expert at most 16 times. In every draw, one expert that a single device serves is named exactly 16 times by every device, and so is the other expert of its index. `slot_expert`: row j holds only 2 * j and 2 * j + 1, each of the two at least once.
All inputs are finite; a program needn't handle non-finite values.
Results may differ from a plain program's by a relative error of at most 0.0065.
Values may be sent and summed in bfloat16 or wider, within the bound.
A program may use at most 128 MiB of HBM per device.

v0:
```python
import jax
import jax.numpy as jnp
from jax import lax
from jax.sharding import PartitionSpec as P

EXP_DEV = 2


def routing(row_experts, slot_expert, replica_here, expert_count):
    matches = slot_expert[None, :, :] == row_experts[:, None, None]
    serve_mask = jnp.sum(matches.astype(jnp.int32), axis=1)
    servers = jnp.sum(serve_mask, axis=1)
    wanted = replica_here % servers + 1
    running = jnp.cumsum(serve_mask, axis=1)
    replica_ids = lax.broadcasted_iota(jnp.int32, serve_mask.shape, 1)
    chosen = (serve_mask == 1) & (running == wanted[:, None])
    target = jnp.sum(jnp.where(chosen, replica_ids, 0), axis=1)
    expert_range = lax.broadcasted_iota(jnp.int32, (row_experts.shape[0], expert_count), 1)
    one_hot = (expert_range == row_experts[:, None]).astype(jnp.int32)
    before = jnp.cumsum(one_hot, axis=0) - one_hot
    row_rank = jnp.sum(before * one_hot, axis=1)
    device_dst = row_experts // EXP_DEV * slot_expert.shape[1] + target
    return (device_dst, row_rank)


def expert_backward(rows_in, rows_grad, gate_matrix, up_matrix, down_matrix):
    gate_pre = jnp.dot(rows_in, gate_matrix, preferred_element_type=jnp.float32)
    up_pre = jnp.dot(rows_in, up_matrix, preferred_element_type=jnp.float32)
    sigmoid_gate = jax.nn.sigmoid(gate_pre)
    silu_gate = gate_pre * sigmoid_gate
    hidden = (silu_gate * up_pre).astype(jnp.bfloat16)
    hidden_grad = jnp.dot(rows_grad, down_matrix, preferred_element_type=jnp.float32)
    up_part = (hidden_grad * silu_gate).astype(jnp.bfloat16)
    gate_part = (
        hidden_grad * up_pre * sigmoid_gate * (1.0 + gate_pre * (1.0 - sigmoid_gate))
    ).astype(jnp.bfloat16)
    contract_hidden = (((1,), (1,)), ((), ()))
    slot_grad = lax.dot_general(
        gate_part, gate_matrix, contract_hidden, preferred_element_type=jnp.float32
    )
    slot_grad = slot_grad + lax.dot_general(
        up_part, up_matrix, contract_hidden, preferred_element_type=jnp.float32
    )
    contract_rows = (((0,), (0,)), ((), ()))
    gate_term = lax.dot_general(
        rows_in, gate_part, contract_rows, preferred_element_type=jnp.float32
    )
    up_term = lax.dot_general(rows_in, up_part, contract_rows, preferred_element_type=jnp.float32)
    down_term = lax.dot_general(
        rows_grad, hidden, contract_rows, preferred_element_type=jnp.float32
    )
    return (slot_grad.astype(jnp.bfloat16), gate_term, up_term, down_term)


def on_device(x_rows, out_grad, gate_weight, up_weight, down_weight, expert_ids, slot_expert):
    expert_here = lax.axis_index("expert")
    replica_here = lax.axis_index("replica")
    n_expert = lax.axis_size("expert")
    n_replica = lax.axis_size("replica")
    rows_here = x_rows.shape[0]
    features = x_rows.shape[1]
    experts_all = EXP_DEV * n_expert
    capacity = max(2, 2 * rows_here // experts_all)
    slot_count = n_expert * n_replica * capacity
    device_dst, row_rank = routing(expert_ids, slot_expert, replica_here, experts_all)
    own_row = lax.dynamic_index_in_dim(slot_expert, expert_here, 0, keepdims=False)
    local_all = own_row - EXP_DEV * expert_here
    replica_range = jnp.arange(n_replica, dtype=jnp.int32)
    local_here = jnp.sum(jnp.where(replica_range == replica_here, local_all, 0))
    server_count = jnp.sum(
        (jnp.arange(EXP_DEV, dtype=jnp.int32)[:, None] == local_all[None, :]).astype(jnp.float32),
        axis=1,
    )[:, None, None]
    send_slot = device_dst * capacity + row_rank
    grad_send = jnp.zeros((slot_count, features), jnp.bfloat16).at[send_slot].set(out_grad)
    input_send = jnp.zeros((slot_count, features), jnp.bfloat16).at[send_slot].set(x_rows)
    grad_send = grad_send.reshape(n_expert, n_replica, capacity, features)
    input_send = input_send.reshape(n_expert, n_replica, capacity, features)
    grad_recv, input_recv = (
        lax.all_to_all(
            lax.all_to_all(grad_send, "expert", split_axis=0, concat_axis=0, tiled=True),
            "replica",
            split_axis=1,
            concat_axis=1,
            tiled=True,
        ),
        lax.all_to_all(
            lax.all_to_all(input_send, "expert", split_axis=0, concat_axis=0, tiled=True),
            "replica",
            split_axis=1,
            concat_axis=1,
            tiled=True,
        ),
    )
    gate_send = jnp.take(gate_weight, local_all, axis=0)
    up_send = jnp.take(up_weight, local_all, axis=0)
    down_send = jnp.take(down_weight, local_all, axis=0)
    gate_full, up_full, down_full = (
        lax.all_to_all(gate_send, "replica", split_axis=0, concat_axis=1, tiled=True),
        lax.all_to_all(up_send, "replica", split_axis=0, concat_axis=1, tiled=True),
        lax.all_to_all(down_send, "replica", split_axis=0, concat_axis=1, tiled=True),
    )
    slot_grad, gate_term, up_term, down_term = expert_backward(
        input_recv.reshape(slot_count, features),
        grad_recv.reshape(slot_count, features),
        gate_full[0],
        up_full[0],
        down_full[0],
    )
    returned = lax.all_to_all(
        lax.all_to_all(
            slot_grad.reshape(n_expert, n_replica, capacity, features),
            "expert",
            split_axis=0,
            concat_axis=0,
            tiled=True,
        ),
        "replica",
        split_axis=1,
        concat_axis=1,
        tiled=True,
    )
    x_grad = returned.reshape(slot_count, features)[send_slot]
    expert_flag = (jnp.arange(EXP_DEV, dtype=jnp.int32) == local_here)[:, None, None]
    gate_sum, up_sum, down_sum = (
        lax.psum_scatter(
            jnp.where(expert_flag, gate_term[None], 0.0).astype(jnp.bfloat16),
            "replica",
            scatter_dimension=1,
            tiled=True,
        ).astype(jnp.float32),
        lax.psum_scatter(
            jnp.where(expert_flag, up_term[None], 0.0).astype(jnp.bfloat16),
            "replica",
            scatter_dimension=1,
            tiled=True,
        ).astype(jnp.float32),
        lax.psum_scatter(
            jnp.where(expert_flag, down_term[None], 0.0).astype(jnp.bfloat16),
            "replica",
            scatter_dimension=1,
            tiled=True,
        ).astype(jnp.float32),
    )
    gate_mean = (gate_sum / server_count).astype(jnp.bfloat16)
    up_mean = (up_sum / server_count).astype(jnp.bfloat16)
    down_mean = (down_sum / server_count).astype(jnp.bfloat16)
    return (x_grad, gate_mean, up_mean, down_mean)


def solution(mesh):
    return jax.shard_map(
        on_device,
        mesh=mesh,
        in_specs=(
            P(("expert", "replica"), None),
            P(("expert", "replica"), None),
            P("expert", "replica", None),
            P("expert", "replica", None),
            P("expert", "replica", None),
            P(("expert", "replica")),
            P(),
        ),
        out_specs=(
            P(("expert", "replica"), None),
            P("expert", "replica", None),
            P("expert", "replica", None),
            P("expert", "replica", None),
        ),
        check_vma=False,
    )
```

profile of v0, /device:TPU:0, one launch (start us, length us, event | category | flops | bytes accessed | tf_op | source)
XLA Modules:
  0.0 814.6 jit_solution(12451690706327037054)
XLA Ops:
  7.2 0.9 fusion.7
  8.0 0.8 convert_reduce_fusion
  9.0 0.8 select_reduce_fusion
  10.0 0.7 compare_select_fusion.1
  10.7 3.6 scatter_custom_fusion.1
  14.3 5.2 all-to-all-start.3
  19.4 3.5 scatter_custom_fusion
  23.0 23.2 %all-to-all-done.3 = bf16[8,4,16,2048]{3,2,1,0:T(8,128)(2,1)} async-done(((bf16[8,4,16,2048]{3,2,1,0:T(8,128)(2,1)}), bf16[8,4,16,2048]{3,2,1,0:T(8,128)(2,1)}, u32[]{:S(2)}, u32[]{:S(2)}) %all-to-all-start.3) | async-done | bytes 2097184 | tf_op jit(solution)/shard_map/all_to_all | solution.py:88
  46.2 4.5 all-to-all-start
  51.5 2.4 gather_fusion.3
  54.0 2.4 gather_fusion.2
  56.4 2.4 gather_fusion.1
  58.8 5.9 broadcast_select_fusion.1
  64.7 12.6 %all-to-all-done = bf16[8,4,16,2048]{3,2,1,0:T(8,128)(2,1)} async-done(((bf16[8,4,16,2048]{3,2,1,0:T(8,128)(2,1)}), bf16[8,4,16,2048]{3,2,1,0:T(8,128)(2,1)}, u32[]{:S(2)}, u32[]{:S(2)}) %all-to-all-start) | async-done | bytes 2097184 | tf_op jit(solution)/shard_map/all_to_all | solution.py:81
  77.3 73.0 %all_to_all.57 = bf16[4,512,768]{2,1,0:T(8,128)(2,1)} all-to-all(bf16[4,512,768]{2,1,0:T(8,128)(2,1)S(1)} %get-tuple-element.17), channel_id=1, replica_groups=mesh['expert'=8,'replica'=4] {'replica'}, dimensions={0} | all-to-all | bytes 6291456 | tf_op jit(solution)/shard_map/all_to_all | solution.py:100
  150.3 3.7 all-to-all-start.6
  154.0 3.2 copy.34
  157.2 65.8 %all-to-all-done.6 = bf16[4,512,768]{2,1,0:T(8,128)(2,1)S(1)} async-done(((bf16[4,512,768]{2,1,0:T(8,128)(2,1)}), bf16[4,512,768]{2,1,0:T(8,128)(2,1)S(1)}, u32[]{:S(2)}, u32[]{:S(2)}) %all-to-all-start.6) | async-done | bytes 3145760 | tf_op jit(solution)/shard_map/all_to_all | solution.py:99
  223.0 1.7 copy-done.6
  224.7 3.6 all-to-all-start.4
  228.3 3.2 copy.32
  231.5 44.4 %all-to-all-done.4 = bf16[8,4,16,2048]{3,2,0,1:T(8,128)(2,1)S(1)} async-done(((bf16[8,4,16,2048]{3,2,0,1:T(8,128)(2,1)}), bf16[8,4,16,2048]{3,2,0,1:T(8,128)(2,1)S(1)}, u32[]{:S(2)}, u32[]{:S(2)}) %all-to-all-start.4) | async-done | bytes 2097184 | tf_op jit(solution)/shard_map/all_to_all | solution.py:87
  275.9 52.1 %all_to_all.58 = bf16[8,4,16,2048]{3,2,0,1:T(8,128)(2,1)} all-to-all(bf16[8,4,16,2048]{3,2,0,1:T(8,128)(2,1)} %copy.32), channel_id=1, replica_groups=mesh['expert'=8,'replica'=4] {'replica'}, dimensions={1} | all-to-all | bytes 4194304 | tf_op jit(solution)/shard_map/all_to_all | solution.py:80
  328.0 4.6 all-to-all-start.2
  333.7 1.4 copy-done.2
  335.4 3.1 copy-done.7
  338.6 1.8 fusion.13
  340.5 1.8 fusion.12
  342.3 1.1 copy-done.17
  343.4 3.6 fusion.5
  347.1 55.4 %all-to-all-done.2 = bf16[4,512,768]{2,1,0:T(8,128)(2,1)} async-done(((bf16[4,512,768]{2,1,0:T(8,128)(2,1)}), bf16[4,512,768]{2,1,0:T(8,128)(2,1)}, u32[]{:S(2)}, u32[]{:S(2)}) %all-to-all-start.2) | async-done | bytes 3145760 | tf_op jit(solution)/shard_map/all_to_all | solution.py:101
  402.5 5.7 multiply_convert_fusion.1
  408.2 1.8 fusion.16
  410.1 1.8 fusion.15
  412.0 7.8 select_convert_fusion
  419.8 0.7 reduce-scatter.6.cloned.1.call-update
  420.6 0.7 reduce-scatter.4.cloned.1.call-update
  421.3 4.0 fusion.14
  425.3 1.8 add_convert_fusion
  427.1 32.6 %all_to_all.59 = bf16[8,4,16,2048]{3,2,1,0:T(8,128)(2,1)S(1)} all-to-all(bf16[8,4,16,2048]{3,2,1,0:T(8,128)(2,1)S(1)} %bitcast.39), channel_id=1, replica_groups=mesh['expert'=8,'replica'=4] {'expert'}, dimensions={0} | all-to-all | bytes 4194304 | tf_op jit(solution)/shard_map/all_to_all | solution.py:111
  459.7 1.5 copy.36
  461.1 4.4 all-to-all-start.8
  465.7 101.2 %all-to-all-done.8 = bf16[8,4,16,2048]{3,2,0,1:T(8,128)(2,1)} async-done(((bf16[8,4,16,2048]{3,2,0,1:T(8,128)(2,1)}), bf16[8,4,16,2048]{3,2,0,1:T(8,128)(2,1)}, u32[]{:S(2)}, u32[]{:S(2)}) %all-to-all-start.8) | async-done | bytes 2097184 | tf_op jit(solution)/shard_map/all_to_all | solution.py:110
  566.9 1.7 copy.37
  568.6 1.7 gather_fusion
  570.4 118.9 %reduce-scatter.6.cloned.1.call-done = bf16[2,512,768]{2,1,0:T(8,128)(2,1)} async-done(((bf16[2,2048,768]{2,1,0:T(8,128)(2,1)}), bf16[2,512,768]{2,1,0:T(8,128)(2,1)}) %reduce-scatter.6.cloned.1.call-update) | async-done | bytes 1572880 | tf_op jit(solution)/shard_map/reduce_scatter | solution.py:132
  689.3 113.6 %reduce-scatter.4.cloned.1.call-done = bf16[2,512,768]{2,1,0:T(8,128)(2,1)} async-done(((bf16[2,2048,768]{2,1,0:T(8,128)(2,1)}), bf16[2,512,768]{2,1,0:T(8,128)(2,1)}) %reduce-scatter.4.cloned.1.call-update) | async-done | bytes 1572880 | tf_op jit(solution)/shard_map/reduce_scatter | solution.py:126
  802.9 5.2 divide_convert_fusion
  (50 shorter events, 2.8 us)
Async XLA Ops:
  7.2 44.3 %copy-start = (bf16[2,512,768]{2,1,0:T(8,128)(2,1)S(1)}, bf16[2,512,768]{2,1,0:T(8,128)(2,1)}, u32[]{:S(2)}) copy-start(bf16[2,512,768]{2,1,0:T(8,128)(2,1)} %param.11) | copy-start | bytes 4718596
  14.3 31.9 %all-to-all-start.3 = ((bf16[8,4,16,2048]{3,2,1,0:T(8,128)(2,1)}), bf16[8,4,16,2048]{3,2,1,0:T(8,128)(2,1)}, u32[]{:S(2)}, u32[]{:S(2)}) async-start(bf16[8,4,16,2048]{3,2,1,0:T(8,128)(2,1)} %bitcast.28), calls=%async_computation.3 | async-start | bytes 4194304 | tf_op jit(solution)/shard_map/all_to_all | solution.py:88
  46.2 4.5 copy-start.12
  46.2 31.1 %all-to-all-start = ((bf16[8,4,16,2048]{3,2,1,0:T(8,128)(2,1)}), bf16[8,4,16,2048]{3,2,1,0:T(8,128)(2,1)}, u32[]{:S(2)}, u32[]{:S(2)}) async-start(bf16[8,4,16,2048]{3,2,1,0:T(8,128)(2,1)} %bitcast.27), calls=%async_computation | async-start | bytes 4194304 | tf_op jit(solution)/shard_map/all_to_all | solution.py:81
  51.5 2.4 copy-start.3
  54.0 2.4 copy-start.4
  150.3 72.7 %all-to-all-start.6 = ((bf16[4,512,768]{2,1,0:T(8,128)(2,1)}), bf16[4,512,768]{2,1,0:T(8,128)(2,1)S(1)}, u32[]{:S(2)}, u32[]{:S(2)}) async-start(bf16[4,512,768]{2,1,0:T(8,128)(2,1)} %get-tuple-element.18), calls=%async_computation.6 | async-start | bytes 6291456 | tf_op jit(solution)/shard_map/all_to_all | solution.py:99
  223.0 1.7 copy-start.6
  224.7 51.3 %all-to-all-start.4 = ((bf16[8,4,16,2048]{3,2,0,1:T(8,128)(2,1)}), bf16[8,4,16,2048]{3,2,0,1:T(8,128)(2,1)S(1)}, u32[]{:S(2)}, u32[]{:S(2)}) async-start(bf16[8,4,16,2048]{3,2,0,1:T(8,128)(2,1)} %copy.34), calls=%async_computation.4 | async-start | bytes 4194304 | tf_op jit(solution)/shard_map/all_to_all | solution.py:87
  328.0 74.4 %all-to-all-start.2 = ((bf16[4,512,768]{2,1,0:T(8,128)(2,1)}), bf16[4,512,768]{2,1,0:T(8,128)(2,1)}, u32[]{:S(2)}, u32[]{:S(2)}) async-start(bf16[4,512,768]{2,1,0:T(8,128)(2,1)} %get-tuple-element.19), calls=%async_computation.2 | async-start | bytes 6291456 | tf_op jit(solution)/shard_map/all_to_all | solution.py:101
  332.7 237.7 %reduce-scatter.8.cloned.1.call-start = ((), (), s32[]{:S(2)}) async-start(), calls=%async_computation.14 | async-start | bytes 7864320 | tf_op jit(solution)/shard_map/reduce_scatter | solution.py:138
  333.6 1.6 copy-start.2
  335.2 5.2 copy-start.9
  335.2 3.4 copy-start.7
  335.4 6.9 copy-start.11
  338.6 1.9 copy-start.5
  340.4 1.9 copy-start.16
  342.3 1.1 copy-start.17
  402.5 5.7 copy-start.10
  408.2 1.9 copy-start.13
  408.2 1.9 copy-start.15
  410.1 1.9 copy-start.8
  419.8 269.5 %reduce-scatter.6.cloned.1.call-start = ((), (), s32[]{:S(2)}) async-start(), calls=%async_computation.13 | async-start | bytes 7864320 | tf_op jit(solution)/shard_map/reduce_scatter | solution.py:132
  420.5 382.4 %reduce-scatter.4.cloned.1.call-start = ((), (), s32[]{:S(2)}) async-start(), calls=%async_computation.12 | async-start | bytes 7864320 | tf_op jit(solution)/shard_map/reduce_scatter | solution.py:126
  421.2 4.0 copy-start.14
  461.1 105.8 %all-to-all-start.8 = ((bf16[8,4,16,2048]{3,2,0,1:T(8,128)(2,1)}), bf16[8,4,16,2048]{3,2,0,1:T(8,128)(2,1)}, u32[]{:S(2)}, u32[]{:S(2)}) async-start(bf16[8,4,16,2048]{3,2,0,1:T(8,128)(2,1)} %copy.36), calls=%async_computation.8 | async-start | bytes 4194304 | tf_op jit(solution)/shard_map/all_to_all | solution.py:110
  802.9 5.2 copy-start.1
Sparse Core Ops, SparseCore 0:
  419.9 144.2 reduce-scatter.7
  566.4 122.8 reduce-scatter.5
  691.6 111.2 reduce-scatter.3
where the time goes:
time: 816 us; the launch traced here: 815 us
  waiting for transfers between devices  537 us (66%)
  blocking collectives  158 us (19%)
  local copies, waits for them, and re-layouts  33.5 us (4%)
  starting transfers between devices  26.3 us (3%)
  other arithmetic  24 us (3%)
  matrix products  22.5 us (3%)
  between operations  14.1 us (2%)
    reduce_scatter x1, waiting for transfers between devices, on_device(): lax.psum_scatter(jnp.where(expert_flag, up_term[None], 0.0).astype(jnp.bf...  119 us
    reduce_scatter x1, waiting for transfers between devices, on_device(): lax.psum_scatter(jnp.where(expert_flag, gate_term[None], 0.0).astype(jnp....  114 us
    all_to_all x1, waiting for transfers between devices, on_device(): lax.all_to_all(lax.all_to_all(slot_grad.reshape(n_expert, n_replica, capa...  101 us
    all_to_all x1, blocking collectives, on_device(): lax.all_to_all(up_send, 'replica', split_axis=0, concat_axis=1, tiled=True)  73 us
    all_to_all x1, waiting for transfers between devices, on_device(): lax.all_to_all(gate_send, 'replica', split_axis=0, concat_axis=1, tiled=T...  65.8 us
    all_to_all x1, waiting for transfers between devices, on_device(): lax.all_to_all(down_send, 'replica', split_axis=0, concat_axis=1, tiled=T...  55.4 us
    all_to_all x1, blocking collectives, on_device(): lax.all_to_all(lax.all_to_all(grad_send, 'expert', split_axis=0, concat_a...  52.1 us
    all_to_all x1, waiting for transfers between devices, on_device(): lax.all_to_all(lax.all_to_all(input_send, 'expert', split_axis=0, concat_...  44.4 us
  transfers between devices with their start and end apart: 9, of which 8 were waited for; matrix products, arithmetic and copies ran while one was open for 5% of the time, Pallas kernels for 0%

commit v1 on v0

v1 whole, which is shorter than its diff:
```python
import jax
import jax.numpy as jnp
from jax import lax
from jax.sharding import PartitionSpec as P

EXP_DEV = 2
BF = jnp.bfloat16
F32 = jnp.float32


def send_slots(row_experts, expert_count, capacity):
    rows = row_experts.shape[0]
    expert_range = lax.broadcasted_iota(jnp.int32, (rows, expert_count), 1)
    one_hot = (expert_range == row_experts[:, None]).astype(BF)
    earlier = lax.broadcasted_iota(jnp.int32, (rows, rows), 1) < lax.broadcasted_iota(
        jnp.int32, (rows, rows), 0
    )
    before = jnp.dot(earlier.astype(BF), one_hot, preferred_element_type=F32)
    rank = jnp.sum(before * one_hot.astype(F32), axis=1)
    return row_experts.astype(F32) * capacity + rank


def middle(rows_in, rows_grad, gate_w, up_w, down_w):
    fwd = (((2,), (1,)), ((0,), (0,)))
    dot = lambda a, b, dims: lax.dot_general(a, b, dims, preferred_element_type=F32)
    partial = jnp.stack(
        [dot(rows_in, gate_w, fwd), dot(rows_in, up_w, fwd), dot(rows_grad, down_w, fwd)]
    ).astype(BF)
    total = lax.psum(partial, "replica").astype(F32)
    gate_pre, up_pre, hidden_grad = total[0], total[1], total[2]
    sig = jax.nn.sigmoid(gate_pre)
    silu = gate_pre * sig
    hidden = (silu * up_pre).astype(BF)
    up_part = (hidden_grad * silu).astype(BF)
    gate_part = (hidden_grad * up_pre * sig * (1.0 + gate_pre * (1.0 - sig))).astype(BF)
    back = (((2,), (2,)), ((0,), (0,)))
    slot_grad = (dot(gate_part, gate_w, back) + dot(up_part, up_w, back)).astype(BF)
    over_rows = (((1,), (1,)), ((0,), (0,)))
    return (
        slot_grad,
        dot(rows_in, gate_part, over_rows),
        dot(rows_in, up_part, over_rows),
        dot(rows_grad, hidden, over_rows),
    )


def on_device(x_rows, out_grad, gate_weight, up_weight, down_weight, expert_ids, slot_expert):
    expert_here = lax.axis_index("expert")
    n_expert = lax.axis_size("expert")
    n_replica = lax.axis_size("replica")
    rows, features = x_rows.shape
    part = features // n_replica
    experts_all = EXP_DEV * n_expert
    capacity = max(2, 2 * rows // experts_all)
    slots = experts_all * capacity
    own_row = lax.dynamic_index_in_dim(slot_expert, expert_here, 0, keepdims=False)
    local_all = own_row - EXP_DEV * expert_here
    servers = jnp.sum(
        (jnp.arange(EXP_DEV, dtype=jnp.int32)[:, None] == local_all[None, :]).astype(F32), axis=1
    )[:, None, None]

    slot_row = send_slots(expert_ids, experts_all, capacity)
    slot_row = jnp.pad(slot_row.astype(BF), (0, part - rows))
    slot_rows = jnp.broadcast_to(slot_row[None, None, :], (n_replica, 16, part))
    split = lambda a: a.reshape(rows, n_replica, part).transpose(1, 0, 2)
    outgoing = jnp.concatenate([split(x_rows), split(out_grad), slot_rows], axis=1)
    arrived = lax.all_to_all(outgoing, "replica", split_axis=0, concat_axis=0, tiled=True)
    slot_of = arrived[:, 2 * rows, :rows].astype(jnp.int32)
    pick = (
        slot_of[:, None, :] == lax.broadcasted_iota(jnp.int32, (n_replica, slots, rows), 1)
    ).astype(BF)
    pairs = arrived[:, : 2 * rows].reshape(n_replica, 2, rows, part)
    packed = jnp.einsum("qsr,qarf->saqf", pick, pairs, preferred_element_type=F32).astype(BF)
    packed = packed.reshape(n_expert, EXP_DEV * capacity, 2, n_replica, part)
    packed = lax.all_to_all(packed, "expert", split_axis=0, concat_axis=0, tiled=True)
    packed = packed.reshape(n_expert, EXP_DEV, capacity, 2, n_replica, part)
    packed = packed.transpose(3, 1, 0, 4, 2, 5).reshape(2, EXP_DEV, -1, part)

    slot_grad, gate_sum, up_sum, down_sum = middle(
        packed[0], packed[1], gate_weight, up_weight, down_weight
    )
    back = slot_grad.reshape(EXP_DEV, n_expert, n_replica, capacity, part).transpose(1, 2, 0, 3, 4)
    back = lax.all_to_all(back, "expert", split_axis=0, concat_axis=0, tiled=True)
    back = back.transpose(1, 0, 2, 3, 4).reshape(n_replica, slots, part)
    x_part = jnp.einsum("qsr,qsf->qrf", pick, back, preferred_element_type=F32).astype(BF)
    x_grad = lax.all_to_all(x_part, "replica", split_axis=0, concat_axis=0, tiled=True)
    x_grad = x_grad.transpose(1, 0, 2).reshape(rows, features)
    mean = lambda total: (total / servers).astype(BF)
    return (x_grad, mean(gate_sum), mean(up_sum), mean(down_sum))


def solution(mesh):
    return jax.shard_map(
        on_device,
        mesh=mesh,
        in_specs=(
            P(("expert", "replica"), None),
            P(("expert", "replica"), None),
            P("expert", "replica", None),
            P("expert", "replica", None),
            P("expert", "replica", None),
            P(("expert", "replica")),
            P(),
        ),
        out_specs=(
            P(("expert", "replica"), None),
            P("expert", "replica", None),
            P("expert", "replica", None),
            P("expert", "replica", None),
        ),
        check_vma=False,
    )
```

time: 816 us -> 310 us (0.38)
  waiting for transfers between devices: 537 us -> 184 us
  blocking collectives: 158 us -> 63.4 us
  local copies, waits for them, and re-layouts: 33.5 us -> 11.5 us
  starting transfers between devices: 26.3 us -> 7.76 us
  other arithmetic: 24 us -> 8.28 us
    all_to_all x6 -> x2, waiting for transfers between devices: 303 us -> 15.7 us  [the longest x1 9.24 us: on_device(): lax.all_to_all(back, 'expert', split_axis=0, concat_axis=0, tiled=True)]
    reduce_scatter x3 -> x0, waiting for transfers between devices: 233 us -> none  [the longest x1 119 us: on_device(): lax.psum_scatter(jnp.where(expert_flag, up_term[None], 0.0).astype(jnp.bf...]
    psum x0 -> x1, waiting for transfers between devices: none -> 168 us  [middle(): total = lax.psum(partial, 'replica').astype(F32)]
    all_to_all x3 -> x2, blocking collectives: 158 us -> 63.4 us  [the longest x1 33.2 us: on_device(): lax.all_to_all(outgoing, 'replica', split_axis=0, concat_axis=0, tiled=True)]
    all_to_all x6 -> x2, starting transfers between devices: 26 us -> 7.72 us  [the longest x1 4.25 us: on_device(): lax.all_to_all(back, 'expert', split_axis=0, concat_axis=0, tiled=True)]
    all_to_all x6 -> x0, local copies, waits for them, and re-layouts: 9.96 us -> none  [the longest x1 3.25 us: on_device(): lax.all_to_all(grad_send, 'expert', split_axis=0, concat_axis=0, tiled=True)]
    gather x4 -> x0, local copies, waits for them, and re-layouts: 8.98 us -> none  [the longest x1 2.44 us: on_device(): gate_send = jnp.take(gate_weight, local_all, axis=0)]
    convert_element_type x3, other arithmetic: 13.8 us -> 5.45 us  [the longest x1 3.18 us: middle(): total = lax.psum(partial, 'replica').astype(F32)]
  transfers between devices with their start and end apart: 9 -> 3, of which waited for: 8 -> 3; matrix products, arithmetic and copies ran while one was open for 5% -> 4% of each run, Pallas kernels for 0% -> 0%
where the time goes in v1:
time: 310 us; the launch traced here: 309 us
  waiting for transfers between devices  184 us (59%)
  blocking collectives  63.4 us (20%)
  matrix products  19.3 us (6%)
  between operations  14.3 us (5%)
  local copies, waits for them, and re-layouts  11.5 us (4%)
  other arithmetic  8.28 us (3%)
  starting transfers between devices  7.76 us (3%)
    psum x1, waiting for transfers between devices, middle(): total = lax.psum(partial, 'replica').astype(F32)  168 us
    all_to_all x1, blocking collectives, on_device(): lax.all_to_all(outgoing, 'replica', split_axis=0, concat_axis=0, tiled=True)  33.2 us
    all_to_all x1, blocking collectives, on_device(): lax.all_to_all(packed, 'expert', split_axis=0, concat_axis=0, tiled=True)  30.1 us
    dot_general x8, matrix products, middle(): lax.dot_general(a, b, dims, preferred_element_type=F32)  16.5 us
    all_to_all x1, waiting for transfers between devices, on_device(): lax.all_to_all(back, 'expert', split_axis=0, concat_axis=0, tiled=True)  9.24 us
    unnamed x23, local copies, waits for them, and re-layouts  6.62 us
    all_to_all x1, waiting for transfers between devices, on_device(): lax.all_to_all(x_part, 'replica', split_axis=0, concat_axis=0, tiled=True)  6.44 us
  transfers between devices with their start and end apart: 3, of which 3 were waited for; matrix products, arithmetic and copies ran while one was open for 4% of the time, Pallas kernels for 0%

profile of v1, /device:TPU:0, one launch (start us, length us, event | category | flops | bytes accessed | tf_op | source)
XLA Modules:
  0.0 308.6 jit_solution(10285102000097194964)
XLA Ops:
  7.2 0.0 copy-start
  7.2 0.0 all-reduce.3.cloned.1.call-start
  7.2 0.9 fusion.4
  8.2 0.7 add_convert_fusion.1
  8.8 1.3 bitcast_bitcast_fusion
  10.2 0.1 pad_maximum_fusion.1
  10.3 33.2 %all_to_all.20 = bf16[4,272,512]{2,1,0:T(8,128)(2,1)S(1)} all-to-all(bf16[4,272,512]{2,1,0:T(8,128)(2,1)S(1)} %pad_maximum_fusion.1), channel_id=1, replica_groups=mesh['expert'=8,'replica'=4] {'replica'}, dimensions={0} | all-to-all | bytes 2228224 | tf_op jit(solution)/shard_map/all_to_all | solution.py:67
  43.5 0.1 slice.31
  43.6 0.8 convolution_convert_fusion
  44.4 0.2 copy.44
  44.7 30.1 %all_to_all.21 = bf16[8,32,2,4,512]{4,1,2,3,0:T(8,128)(2,1)S(1)} all-to-all(bf16[8,32,2,4,512]{4,1,2,3,0:T(8,128)(2,1)S(1)} %copy.44), channel_id=1, replica_groups=mesh['expert'=8,'replica'=4] {'expert'}, dimensions={0} | all-to-all | bytes 4194304 | tf_op jit(solution)/shard_map/all_to_all | solution.py:75
  74.8 0.2 copy.65
  75.0 0.0 copy-start.3
  75.1 0.3 fusion.14
  75.3 0.0 copy-start.7
  75.3 1.5 copy-done.3
  76.9 1.0 fusion.2
  77.9 0.0 copy-done.7
  77.9 0.0 copy-start.10
  77.9 1.0 fusion.1
  78.9 0.4 copy-done.10
  79.3 1.0 fusion.3
  80.3 2.4 pad_maximum_fusion
  82.7 0.0 all-reduce.3.cloned.1.call-update
  82.7 0.7 copy-done.9
  83.4 0.2 subtract_reduce_fusion
  83.6 0.1 fusion.12
  83.7 168.4 %all-reduce.3.cloned.1.call-done = bf16[3,2,512,768]{3,2,1,0:T(8,128)(2,1)} async-done(((bf16[3,2,512,768]{3,2,1,0:T(8,128)(2,1)}), bf16[3,2,512,768]{3,2,1,0:T(8,128)(2,1)}) %all-reduce.3.cloned.1.call-update) | async-done | bytes 4718608 | tf_op jit(solution)/shard_map/psum | solution.py:29
  252.1 3.2 %convert_element_type.61 = f32[3,2,512,768]{3,2,1,0:T(8,128)S(1)} convert(bf16[3,2,512,768]{3,2,1,0:T(8,128)(2,1)} %all-reduce.3.cloned.1.call-done) | non-fusion elementwise | flops 2359296 | bytes 14155776 | tf_op jit(solution)/shard_map/convert_element_type | solution.py:29
  255.3 1.6 multiply_convert_fusion.1
  256.9 2.0 copy-done.1
  258.9 1.0 fusion.15
  259.9 0.1 copy-done.2
  260.0 0.8 copy-done.4
  260.9 1.0 add_convert_fusion
  261.9 1.1 copy.66
  263.0 4.2 %all-to-all-start.2 = ((bf16[8,4,2,16,512]{4,3,1,2,0:T(8,128)(2,1)}), bf16[8,4,2,16,512]{4,3,1,2,0:T(8,128)(2,1)}, u32[]{:S(2)}, u32[]{:S(2)}) async-start(bf16[8,4,2,16,512]{4,3,1,2,0:T(8,128)(2,1)} %bitcast.84), calls=%async_computation.2 | async-start | bytes 2097152 | tf_op jit(solution)/shard_map/all_to_all | solution.py:83
  267.2 0.0 copy-start.8
  267.2 4.0 %divide_convert_fusion.1 = bf16[2,512,768]{2,1,0:T(8,128)(2,1)} fusion(bf16[2,512,512]{2,1,0:T(8,128)(2,1)} %bitcast.94, bf16[2,512,768]{2,1,0:T(8,128)(2,1)} %copy-done.2, f32[2]{0:T(128)S(1)} %fusion.12), kind=kOutput, calls=%fused_computation.6 | convolution fusion | flops 806879232 | bytes 4194312 | tf_op jit(solution)/shard_map/dot_general | solution.py:25
  271.2 2.2 divide_convert_fusion.2
  273.4 9.2 %all-to-all-done.2 = bf16[8,4,2,16,512]{4,3,1,2,0:T(8,128)(2,1)} async-done(((bf16[8,4,2,16,512]{4,3,1,2,0:T(8,128)(2,1)}), bf16[8,4,2,16,512]{4,3,1,2,0:T(8,128)(2,1)}, u32[]{:S(2)}, u32[]{:S(2)}) %all-to-all-start.2) | async-done | bytes 1048608 | tf_op jit(solution)/shard_map/all_to_all | solution.py:83
  282.6 1.4 copy.47
  284.0 1.1 convolution_convert_fusion.4
  285.2 3.5 %all-to-all-start.3 = ((bf16[4,128,512]{2,1,0:T(8,128)(2,1)}), bf16[4,128,512]{2,1,0:T(8,128)(2,1)S(1)}, u32[]{:S(2)}, u32[]{:S(2)}) async-start(bf16[4,128,512]{2,1,0:T(8,128)(2,1)} %convolution_convert_fusion.4), calls=%async_computation.3 | async-start | bytes 1048576 | tf_op jit(solution)/shard_map/all_to_all | solution.py:86
  288.7 5.3 %divide_convert_fusion = bf16[2,512,768]{2,1,0:T(8,128)(2,1)} fusion(bf16[2,512,512]{2,1,0:T(8,128)(2,1)S(1)} %bitcast.91, f32[3,2,512,768]{3,2,1,0:T(8,128)} %copy-done.1, f32[2]{0:T(128)S(1)} %fusion.12), kind=kOutput, calls=%fused_computation.4 | convolution fusion | flops 811597824 | bytes 8912904 | tf_op jit(solution)/shard_map/dot_general | solution.py:25
  294.0 6.4 %all-to-all-done.3 = bf16[4,128,512]{2,1,0:T(8,128)(2,1)S(1)} async-done(((bf16[4,128,512]{2,1,0:T(8,128)(2,1)}), bf16[4,128,512]{2,1,0:T(8,128)(2,1)S(1)}, u32[]{:S(2)}, u32[]{:S(2)}) %all-to-all-start.3) | async-done | bytes 524320 | tf_op jit(solution)/shard_map/all_to_all | solution.py:86
  300.4 0.3 copy.48
  300.7 1.0 copy.52
  (13 shorter events, 0.0 us)
Async XLA Ops:
  7.2 70.7 %copy-start = (bf16[2,512,768]{2,1,0:T(8,128)(2,1)S(1)}, bf16[2,512,768]{2,1,0:T(8,128)(2,1)}, u32[]{:S(2)}) copy-start(bf16[2,512,768]{2,1,0:T(8,128)(2,1)} %param.9) | copy-start | bytes 4718596
  7.2 244.9 %all-reduce.3.cloned.1.call-start = ((), (), s32[]{:S(2)}) async-start(), calls=%async_computation.4 | async-start | bytes 9437184 | tf_op jit(solution)/shard_map/psum | solution.py:29
  75.0 1.8 copy-start.3
  75.3 2.5 copy-start.7
  75.3 3.6 %copy-start.5 = (bf16[1,2,8,4,16,512]{5,4,3,2,1,0:T(8,128)(2,1)}, bf16[1,2,8,4,16,512]{5,4,3,2,1,0:T(8,128)(2,1)S(1)}, u32[]{:S(2)}) copy-start(bf16[1,2,8,4,16,512]{5,4,3,2,1,0:T(8,128)(2,1)S(1)} %get-tuple-element.19) | copy-start | bytes 3145732
  77.9 1.4 copy-start.10
  82.7 0.7 copy-start.9
  255.3 3.6 %copy-start.1 = (f32[3,2,512,768]{3,2,1,0:T(8,128)}, f32[3,2,512,768]{3,2,1,0:T(8,128)S(1)}, u32[]{:S(2)}) copy-start(f32[3,2,512,768]{3,2,1,0:T(8,128)S(1)} %convert_element_type.61) | copy-start | bytes 28311556
  258.9 1.1 copy-start.2
  258.9 2.0 copy-start.4
  263.0 19.7 %all-to-all-start.2 = ((bf16[8,4,2,16,512]{4,3,1,2,0:T(8,128)(2,1)}), bf16[8,4,2,16,512]{4,3,1,2,0:T(8,128)(2,1)}, u32[]{:S(2)}, u32[]{:S(2)}) async-start(bf16[8,4,2,16,512]{4,3,1,2,0:T(8,128)(2,1)} %bitcast.84), calls=%async_computation.2 | async-start | bytes 2097152 | tf_op jit(solution)/shard_map/all_to_all | solution.py:83
  267.2 4.0 %copy-start.8 = (bf16[1,2,8,4,16,512]{5,4,3,2,1,0:T(8,128)(2,1)S(1)}, bf16[1,2,8,4,16,512]{5,4,3,2,1,0:T(8,128)(2,1)}, u32[]{:S(2)}) copy-start(bf16[1,2,8,4,16,512]{5,4,3,2,1,0:T(8,128)(2,1)} %copy-done.7) | copy-start | bytes 3145732
  282.6 6.0 %copy-start.6 = (bf16[1,2,8,4,16,512]{5,4,3,2,1,0:T(8,128)(2,1)S(1)}, bf16[1,2,8,4,16,512]{5,4,3,2,1,0:T(8,128)(2,1)}, u32[]{:S(2)}) copy-start(bf16[1,2,8,4,16,512]{5,4,3,2,1,0:T(8,128)(2,1)} %copy-done.5) | copy-start | bytes 3145732
  285.2 15.3 %all-to-all-start.3 = ((bf16[4,128,512]{2,1,0:T(8,128)(2,1)}), bf16[4,128,512]{2,1,0:T(8,128)(2,1)S(1)}, u32[]{:S(2)}, u32[]{:S(2)}) async-start(bf16[4,128,512]{2,1,0:T(8,128)(2,1)} %convolution_convert_fusion.4), calls=%async_computation.3 | async-start | bytes 1048576 | tf_op jit(solution)/shard_map/all_to_all | solution.py:86
Sparse Core Ops, SparseCore 0:
  82.9 169.1 all-reduce.2

commit v2 on v1

--- a/solution.py
+++ b/solution.py
@@ -1,6 +1,10 @@
+import functools
+
 import jax
 import jax.numpy as jnp
 from jax import lax
+from jax.experimental import pallas as pl
+from jax.experimental.pallas import tpu as pltpu
 from jax.sharding import PartitionSpec as P
 
 EXP_DEV = 2
@@ -20,19 +24,178 @@
     return row_experts.astype(F32) * capacity + rank
 
 
-def middle(rows_in, rows_grad, gate_w, up_w, down_w):
-    fwd = (((2,), (1,)), ((0,), (0,)))
+def line_kernel(
+    n_replica, x_ref, g_ref, a_ref, b_ref, c_ref, gate_ref, up_ref, hid_ref,
+    own, from_left, from_right, to_right, to_left, total, send_r, recv_r, send_l, recv_l,
+):
+    here = lax.axis_index("replica")
+    last = n_replica - 1
+    n_chunk, chunk, _ = own.shape
+    hidden = a_ref.shape[2]
+    rows = x_ref.shape[1]
+    block = min(128, rows)
+    per_block = block // chunk
+
+    def rightward(c):
+        return pltpu.make_async_remote_copy(
+            src_ref=to_right.at[c], dst_ref=from_left.at[c],
+            send_sem=send_r.at[c], recv_sem=recv_r.at[c],
+            device_id={"replica": lax.rem(here + 1, n_replica)},
+            device_id_type=pl.DeviceIdType.MESH,
+        )
+
+    def leftward(c):
+        return pltpu.make_async_remote_copy(
+            src_ref=to_left.at[c], dst_ref=from_right.at[c],
+            send_sem=send_l.at[c], recv_sem=recv_l.at[c],
+            device_id={"replica": lax.rem(here + last, n_replica)},
+            device_id_type=pl.DeviceIdType.MESH,
+        )
+
+    barrier = pltpu.get_barrier_semaphore()
+
+    @pl.when(here > 0)
+    def _():
+        pl.semaphore_signal(
+            barrier, inc=1, device_id={"replica": lax.rem(here + last, n_replica)},
+            device_id_type=pl.DeviceIdType.MESH,
+        )
+
+    @pl.when(here < last)
+    def _():
+        pl.semaphore_signal(
+            barrier, inc=1, device_id={"replica": lax.rem(here + 1, n_replica)},
+            device_id_type=pl.DeviceIdType.MESH,
+        )
+
+    @pl.when((here > 0) & (here < last))
+    def _():
+        pl.semaphore_wait(barrier, 2)
+
+    @pl.when((here == 0) | (here == last))
+    def _():
+        pl.semaphore_wait(barrier, 1)
+
+    for e in range(EXP_DEV):
+
+        @pl.loop(0, rows // block)
+        def _(b):
+            at = pl.ds(pl.multiple_of(b * block, block), block)
+            first = e * (rows // chunk) + b * per_block
+            for w, (lhs, rhs) in enumerate(((x_ref, a_ref), (x_ref, b_ref), (g_ref, c_ref))):
+                part = jnp.dot(lhs[e, at, :], rhs[e], preferred_element_type=F32)
+                own[pl.ds(first, per_block), :, w * hidden : (w + 1) * hidden] = part.reshape(
+                    per_block, chunk, hidden
+                )
+            for k in range(per_block):
+
+                @pl.when(here == 0)
+                def _():
+                    to_right[first + k] = own[first + k].astype(BF)
+                    rightward(first + k).start()
+
+                @pl.when(here == last)
+                def _():
+                    to_left[first + k] = own[first + k].astype(BF)
+                    leftward(first + k).start()
+
+    @pl.loop(0, n_chunk + last)
+    def _(t):
+        c_left = t - here
+        c_right = t - (last - here)
+        done = t - last
+
+        @pl.when((here > 0) & (c_left >= 0) & (c_left < n_chunk))
+        def _():
+            rightward(c_left).wait_recv()
+
+            @pl.when(here < last)
+            def _():
+                to_right[c_left] = (own[c_left] + from_left[c_left].astype(F32)).astype(BF)
+                rightward(c_left).start()
+
+        @pl.when((here < last) & (c_right >= 0) & (c_right < n_chunk))
+        def _():
+            leftward(c_right).wait_recv()
+
+            @pl.when(here > 0)
+            def _():
+                to_left[c_right] = (own[c_right] + from_right[c_right].astype(F32)).astype(BF)
+                leftward(c_right).start()
+
+        @pl.when(done >= 0)
+        def _():
+            total[...] = own[done]
+
+            @pl.when(here > 0)
+            def _():
+                total[...] += from_left[done].astype(F32)
+
+            @pl.when(here < last)
+            def _():
+                total[...] += from_right[done].astype(F32)
+
+            gate_pre = total[:, :hidden]
+            up_pre = total[:, hidden : 2 * hidden]
+            hidden_grad = total[:, 2 * hidden :]
+            sig = jax.nn.sigmoid(gate_pre)
+            silu = gate_pre * sig
+            hid_ref[done] = (silu * up_pre).astype(BF)
+            up_ref[done] = (hidden_grad * silu).astype(BF)
+            gate_ref[done] = (
+                hidden_grad * up_pre * sig * (1.0 + gate_pre * (1.0 - sig))
+            ).astype(BF)
+
+    @pl.loop(0, n_chunk)
+    def _(c):
+        @pl.when(here < last)
+        def _():
+            rightward(c).wait_send()
+
+        @pl.when(here > 0)
+        def _():
+            leftward(c).wait_send()
+
+
+def hidden_parts(n_replica, rows_in, rows_grad, gate_w, up_w, down_w):
+    rows, part = rows_in.shape[1:]
+    hidden = gate_w.shape[2]
+    chunk = min(32, rows)
+    n_chunk = EXP_DEV * rows // chunk
+    wide = (n_chunk, chunk, 3 * hidden)
+    vmem = pl.BlockSpec(memory_space=pltpu.VMEM)
+    outs = pl.pallas_call(
+        functools.partial(line_kernel, n_replica),
+        out_shape=[jax.ShapeDtypeStruct((n_chunk, chunk, hidden), BF)] * 3,
+        in_specs=[vmem] * 5,
+        out_specs=[vmem] * 3,
+        scratch_shapes=[
+            pltpu.VMEM(wide, F32),
+            pltpu.VMEM(wide, BF),
+            pltpu.VMEM(wide, BF),
+            pltpu.VMEM(wide, BF),
+            pltpu.VMEM(wide, BF),
+            pltpu.VMEM(wide[1:], F32),
+            pltpu.SemaphoreType.DMA((n_chunk,)),
+            pltpu.SemaphoreType.DMA((n_chunk,)),
+            pltpu.SemaphoreType.DMA((n_chunk,)),
+            pltpu.SemaphoreType.DMA((n_chunk,)),
+        ],
+        compiler_params=pltpu.CompilerParams(
+            collective_id=0, has_side_effects=True, vmem_limit_bytes=54 * 2**20
+        ),
+        cost_estimate=pl.CostEstimate(
+            flops=6 * EXP_DEV * rows * part * hidden, bytes_accessed=2**24, transcendentals=2**20
+        ),
+    )(rows_in, rows_grad, gate_w, up_w, down_w)
+    return [o.reshape(EXP_DEV, rows, hidden) for o in outs]
+
+
+def middle(n_replica, rows_in, rows_grad, gate_w, up_w, down_w):
+    gate_part, up_part, hidden = hidden_parts(
+        n_replica, rows_in, rows_grad, gate_w, up_w, down_w
+    )
     dot = lambda a, b, dims: lax.dot_general(a, b, dims, preferred_element_type=F32)
-    partial = jnp.stack(
-        [dot(rows_in, gate_w, fwd), dot(rows_in, up_w, fwd), dot(rows_grad, down_w, fwd)]
-    ).astype(BF)
-    total = lax.psum(partial, "replica").astype(F32)
-    gate_pre, up_pre, hidden_grad = total[0], total[1], total[2]
-    sig = jax.nn.sigmoid(gate_pre)
-    silu = gate_pre * sig
-    hidden = (silu * up_pre).astype(BF)
-    up_part = (hidden_grad * silu).astype(BF)
-    gate_part = (hidden_grad * up_pre * sig * (1.0 + gate_pre * (1.0 - sig))).astype(BF)
     back = (((2,), (2,)), ((0,), (0,)))
     slot_grad = (dot(gate_part, gate_w, back) + dot(up_part, up_w, back)).astype(BF)
     over_rows = (((1,), (1,)), ((0,), (0,)))
@@ -77,7 +240,7 @@
     packed = packed.transpose(3, 1, 0, 4, 2, 5).reshape(2, EXP_DEV, -1, part)
 
     slot_grad, gate_sum, up_sum, down_sum = middle(
-        packed[0], packed[1], gate_weight, up_weight, down_weight
+        n_replica, packed[0], packed[1], gate_weight, up_weight, down_weight
     )
     back = slot_grad.reshape(EXP_DEV, n_expert, n_replica, capacity, part).transpose(1, 2, 0, 3, 4)
     back = lax.all_to_all(back, "expert", split_axis=0, concat_axis=0, tiled=True)

time: 310 us -> 241 us (0.78)
  waiting for transfers between devices: 184 us -> 17.9 us
  Pallas kernels: 0 us -> 121 us
  between operations: 14.3 us -> 0.81 us
  other arithmetic: 8.28 us -> 1.09 us
  starting transfers between devices: 7.76 us -> 13.3 us
  local copies, waits for them, and re-layouts: 11.5 us -> 6.51 us
  matrix products: 19.3 us -> 15.6 us
    psum x1 -> x0, waiting for transfers between devices: 168 us -> none  [middle(): total = lax.psum(partial, 'replica').astype(F32)]
    pallas_call x0 -> x1, Pallas kernels: none -> 121 us  [hidden_parts(): pl.pallas_call(functools.partial(line_kernel, n_replica), out_shape=[jax....]
    unnamed x23 -> x15, local copies, waits for them, and re-layouts: 6.62 us -> 1.04 us
    all_to_all x1, starting transfers between devices: 4.25 us -> 9.82 us  [on_device(): lax.all_to_all(back, 'expert', split_axis=0, concat_axis=0, tiled=True)]
    convert_element_type x2 -> x0, other arithmetic: 4.77 us -> none  [the longest x1 3.18 us: middle(): total = lax.psum(partial, 'replica').astype(F32)]
    dot_general x8 -> x5, matrix products: 16.5 us -> 12.7 us  [middle(): lax.dot_general(a, b, dims, preferred_element_type=F32)]
  transfers between devices with their start and end apart: 3 -> 2, of which waited for: 3 -> 2; matrix products, arithmetic and copies ran while one was open for 4% -> 4% of each run, Pallas kernels for 0% -> 0%
where the time goes in v2:
time: 241 us; the launch traced here: 240 us
  Pallas kernels  121 us (50%)
  blocking collectives  63.4 us (26%)
  waiting for transfers between devices  17.9 us (7%)
  matrix products  15.6 us (6%)
  starting transfers between devices  13.3 us (6%)
  local copies, waits for them, and re-layouts  6.51 us (3%)
    pallas_call x1, Pallas kernels, hidden_parts(): pl.pallas_call(functools.partial(line_kernel, n_replica), out_shape=[jax....  121 us
    all_to_all x1, blocking collectives, on_device(): lax.all_to_all(outgoing, 'replica', split_axis=0, concat_axis=0, tiled=True)  33.2 us
    all_to_all x1, blocking collectives, on_device(): lax.all_to_all(packed, 'expert', split_axis=0, concat_axis=0, tiled=True)  30.1 us
    dot_general x5, matrix products, middle(): lax.dot_general(a, b, dims, preferred_element_type=F32)  12.7 us
    all_to_all x1, waiting for transfers between devices, on_device(): lax.all_to_all(back, 'expert', split_axis=0, concat_axis=0, tiled=True)  11.7 us
    all_to_all x1, starting transfers between devices, on_device(): lax.all_to_all(back, 'expert', split_axis=0, concat_axis=0, tiled=True)  9.82 us
    all_to_all x1, waiting for transfers between devices, on_device(): lax.all_to_all(x_part, 'replica', split_axis=0, concat_axis=0, tiled=True)  6.15 us
  transfers between devices with their start and end apart: 2, of which 2 were waited for; matrix products, arithmetic and copies ran while one was open for 4% of the time, Pallas kernels for 0%

profile of v2, /device:TPU:0, one launch (start us, length us, event | category | flops | bytes accessed | tf_op | source)
XLA Modules:
  0.0 239.6 jit_solution(8829576902700413555)
XLA Ops:
  0.6 0.9 fusion
  1.5 0.7 add_convert_fusion.1
  2.2 1.3 bitcast_bitcast_fusion
  3.5 0.1 pad_maximum_fusion
  3.6 33.2 %all_to_all.20 = bf16[4,272,512]{2,1,0:T(8,128)(2,1)S(1)} all-to-all(bf16[4,272,512]{2,1,0:T(8,128)(2,1)S(1)} %pad_maximum_fusion), channel_id=1, replica_groups=mesh['expert'=8,'replica'=4] {'replica'}, dimensions={0} | all-to-all | bytes 2228224 | tf_op jit(solution)/shard_map/all_to_all | solution.py:230
  36.9 0.1 slice.19
  37.0 0.8 convolution_convert_fusion
  37.8 0.2 copy.46
  38.0 30.1 %all_to_all.21 = bf16[8,32,2,4,512]{4,1,3,2,0:T(8,128)(2,1)S(1)} all-to-all(bf16[8,32,2,4,512]{4,1,3,2,0:T(8,128)(2,1)S(1)} %copy.46), channel_id=1, replica_groups=mesh['expert'=8,'replica'=4] {'expert'}, dimensions={0} | all-to-all | bytes 4194304 | tf_op jit(solution)/shard_map/all_to_all | solution.py:238
  68.2 0.3 fusion.8
  68.4 1.1 copy.48
  69.5 1.1 copy.47
  70.6 0.0 copy-start
  70.6 121.1 %shard_map.102 = (bf16[32,32,768]{2,1,0:T(8,128)(2,1)}, bf16[32,32,768]{2,1,0:T(8,128)(2,1)}, bf16[32,32,768]{2,1,0:T(8,128)(2,1)}) custom-call(bf16[2,512,512]{2,1,0:T(8,128)(2,1)} %bitcast.62, bf16[2,512,512]{2,1,0:T(8,128)(2,1)} %bitcast.60, bf16[2,512,768]{2,1,0:T(8,128)(2,1)} %a_ref.1, bf16[2,512,768]{2,1,0:T(8,128)(2,1)} %b_ref.1, ...), custom_call_target="tpu_custom_call" | custom-call | flops 2415919104 | bytes 16777216 | tf_op jit(solution)/shard_map/pallas_call | solution.py:167
  191.7 0.0 copy-done
  191.7 0.0 copy-start.1
  191.7 0.0 copy-start.3
  191.7 2.6 %fusion.9 = f32[2,512,512]{2,1,0:T(8,128)S(1)} fusion(bf16[2,512,768]{2,1,0:T(8,128)(2,1)} %bitcast.56, bf16[2,512,768]{2,1,0:T(8,128)(2,1)S(1)} %copy-done), kind=kOutput, calls=%fused_computation.26 | convolution fusion | flops 805306368 | bytes 5242880 | tf_op jit(solution)/shard_map/dot_general | solution.py:198
  194.3 0.0 copy-done.1
  194.3 0.0 copy-done.3
  194.3 1.0 add_convert_fusion
  195.4 1.0 copy.67
  196.4 0.0 copy-start.5
  196.4 9.8 %all-to-all-start.2 = ((bf16[8,4,2,16,512]{4,3,1,2,0:T(8,128)(2,1)}), bf16[8,4,2,16,512]{4,3,1,2,0:T(8,128)(2,1)S(1)}, u32[]{:S(2)}, u32[]{:S(2)}) async-start(bf16[8,4,2,16,512]{4,3,1,2,0:T(8,128)(2,1)} %bitcast.47), calls=%async_computation.2 | async-start | bytes 2097152 | tf_op jit(solution)/shard_map/all_to_all | solution.py:246
  206.2 0.0 copy-done.5
  206.2 0.2 subtract_reduce_fusion
  206.4 0.1 fusion.7
  206.5 3.4 %divide_convert_fusion.1 = bf16[2,512,768]{2,1,0:T(8,128)(2,1)} fusion(bf16[2,512,512]{2,1,0:T(8,128)(2,1)} %bitcast.63, bf16[2,512,768]{2,1,0:T(8,128)(2,1)S(1)} %bitcast.59, f32[2]{0:T(128)S(1)} %fusion.7), kind=kOutput, calls=%fused_computation.1 | convolution fusion | flops 806879232 | bytes 4194312 | tf_op jit(solution)/shard_map/dot_general | solution.py:198
  209.9 11.7 %all-to-all-done.2 = bf16[8,4,2,16,512]{4,3,1,2,0:T(8,128)(2,1)S(1)} async-done(((bf16[8,4,2,16,512]{4,3,1,2,0:T(8,128)(2,1)}), bf16[8,4,2,16,512]{4,3,1,2,0:T(8,128)(2,1)S(1)}, u32[]{:S(2)}, u32[]{:S(2)}) %all-to-all-start.2) | async-done | bytes 1048608 | tf_op jit(solution)/shard_map/all_to_all | solution.py:246
  221.6 0.1 copy.50
  221.7 0.0 copy-start.2
  221.7 1.2 convolution_convert_fusion.1
  222.9 3.5 %all-to-all-start.3 = ((bf16[4,128,512]{2,1,0:T(8,128)(2,1)}), bf16[4,128,512]{2,1,0:T(8,128)(2,1)S(1)}, u32[]{:S(2)}, u32[]{:S(2)}) async-start(bf16[4,128,512]{2,1,0:T(8,128)(2,1)} %convolution_convert_fusion.1), calls=%async_computation.3 | async-start | bytes 1048576 | tf_op jit(solution)/shard_map/all_to_all | solution.py:249
  226.4 0.0 copy-done.2
  226.4 0.0 copy-start.4
  226.4 0.0 copy-start.6
  226.4 3.5 %divide_convert_fusion.2 = bf16[2,512,768]{2,1,0:T(8,128)(2,1)} fusion(bf16[2,512,512]{2,1,0:T(8,128)(2,1)} %bitcast.64, bf16[2,512,768]{2,1,0:T(8,128)(2,1)S(1)} %bitcast.57, f32[2]{0:T(128)S(1)} %fusion.7), kind=kOutput, calls=%fused_computation.2 | convolution fusion | flops 806879232 | bytes 4194312 | tf_op jit(solution)/shard_map/dot_general | solution.py:198
  229.9 0.0 copy-done.4
  230.0 0.0 copy-done.6
  230.0 2.2 divide_convert_fusion
  232.2 6.2 %all-to-all-done.3 = bf16[4,128,512]{2,1,0:T(8,128)(2,1)S(1)} async-done(((bf16[4,128,512]{2,1,0:T(8,128)(2,1)}), bf16[4,128,512]{2,1,0:T(8,128)(2,1)S(1)}, u32[]{:S(2)}, u32[]{:S(2)}) %all-to-all-start.3) | async-done | bytes 524320 | tf_op jit(solution)/shard_map/all_to_all | solution.py:249
  238.3 0.3 copy.51
  238.6 1.0 copy.55
  (3 shorter events, 0.0 us)
Async XLA Ops:
  70.6 121.1 %copy-start = (bf16[2,512,768]{2,1,0:T(8,128)(2,1)S(1)}, bf16[2,512,768]{2,1,0:T(8,128)(2,1)}, u32[]{:S(2)}) copy-start(bf16[2,512,768]{2,1,0:T(8,128)(2,1)} %a_ref.1) | copy-start | bytes 4718596
  191.7 2.6 %copy-start.1 = (bf16[2,512,768]{2,1,0:T(8,128)(2,1)S(1)}, bf16[2,512,768]{2,1,0:T(8,128)(2,1)}, u32[]{:S(2)}) copy-start(bf16[2,512,768]{2,1,0:T(8,128)(2,1)} %b_ref.1) | copy-start | bytes 4718596
  191.7 2.6 %copy-start.3 = (bf16[32,32,768]{2,1,0:T(8,128)(2,1)S(1)}, bf16[32,32,768]{2,1,0:T(8,128)(2,1)}, u32[]{:S(2)}) copy-start(bf16[32,32,768]{2,1,0:T(8,128)(2,1)} %get-tuple-element.8) | copy-start | bytes 4718596
  196.4 9.8 %copy-start.5 = (s32[8,4]{0,1:T(4,128)S(1)}, s32[8,4]{0,1:T(4,128)}, u32[]{:S(2)}) copy-start(s32[8,4]{0,1:T(4,128)} %param.13) | copy-start | bytes 388
  196.4 25.2 %all-to-all-start.2 = ((bf16[8,4,2,16,512]{4,3,1,2,0:T(8,128)(2,1)}), bf16[8,4,2,16,512]{4,3,1,2,0:T(8,128)(2,1)S(1)}, u32[]{:S(2)}, u32[]{:S(2)}) async-start(bf16[8,4,2,16,512]{4,3,1,2,0:T(8,128)(2,1)} %bitcast.47), calls=%async_computation.2 | async-start | bytes 2097152 | tf_op jit(solution)/shard_map/all_to_all | solution.py:246
  221.7 4.6 %copy-start.2 = (bf16[32,32,768]{2,1,0:T(8,128)(2,1)S(1)}, bf16[32,32,768]{2,1,0:T(8,128)(2,1)}, u32[]{:S(2)}) copy-start(bf16[32,32,768]{2,1,0:T(8,128)(2,1)} %get-tuple-element.7) | copy-start | bytes 4718596
  222.9 15.4 %all-to-all-start.3 = ((bf16[4,128,512]{2,1,0:T(8,128)(2,1)}), bf16[4,128,512]{2,1,0:T(8,128)(2,1)S(1)}, u32[]{:S(2)}, u32[]{:S(2)}) async-start(bf16[4,128,512]{2,1,0:T(8,128)(2,1)} %convolution_convert_fusion.1), calls=%async_computation.3 | async-start | bytes 1048576 | tf_op jit(solution)/shard_map/all_to_all | solution.py:249
  226.4 3.6 %copy-start.4 = (bf16[1,2,8,4,16,512]{5,4,3,2,1,0:T(8,128)(2,1)S(1)}, bf16[1,2,8,4,16,512]{5,4,3,2,1,0:T(8,128)(2,1)}, u32[]{:S(2)}) copy-start(bf16[1,2,8,4,16,512]{5,4,3,2,1,0:T(8,128)(2,1)} %copy.48) | copy-start | bytes 3145732
  226.4 3.6 %copy-start.6 = (bf16[32,32,768]{2,1,0:T(8,128)(2,1)S(1)}, bf16[32,32,768]{2,1,0:T(8,128)(2,1)}, u32[]{:S(2)}) copy-start(bf16[32,32,768]{2,1,0:T(8,128)(2,1)} %get-tuple-element.9) | copy-start | bytes 4718596

commit v3 on v2

v3 whole, which is shorter than its diff:
```python
import functools

import jax
import jax.numpy as jnp
from jax import lax
from jax.experimental import pallas as pl
from jax.experimental.pallas import tpu as pltpu
from jax.sharding import PartitionSpec as P

EXP_DEV = 2
BF = jnp.bfloat16
F32 = jnp.float32


def send_slots(row_experts, expert_count, capacity):
    rows = row_experts.shape[0]
    expert_range = lax.broadcasted_iota(jnp.int32, (rows, expert_count), 1)
    one_hot = (expert_range == row_experts[:, None]).astype(BF)
    earlier = lax.broadcasted_iota(jnp.int32, (rows, rows), 1) < lax.broadcasted_iota(
        jnp.int32, (rows, rows), 0
    )
    before = jnp.dot(earlier.astype(BF), one_hot, preferred_element_type=F32)
    rank = jnp.sum(before * one_hot.astype(F32), axis=1)
    return row_experts.astype(F32) * capacity + rank


HOP_STEPS = 2


def flip(index, other, size):
    result, bit = 0, 1
    while bit < size:
        result = result + lax.rem(index // bit + other // bit, 2) * bit
        bit *= 2
    return result


def line_kernel(
    n_expert, n_replica, packed, a_ref, b_ref, c_ref, pairs, ret, gate_ref, up_ref, hid_ref,
    own, from_left, from_right, to_right, to_left, back, total,
    send_r, recv_r, send_l, recv_l, send_p, recv_p, send_b, recv_b,
):
    here = lax.axis_index("replica")
    index = lax.axis_index("expert")
    last = n_replica - 1
    n_chunk, chunk, _ = own.shape
    hidden = a_ref.shape[2]
    rows = packed.shape[2]
    per_source = rows // chunk
    per_expert = rows // EXP_DEV
    mesh_id = pl.DeviceIdType.MESH

    def rightward(c):
        return pltpu.make_async_remote_copy(
            src_ref=to_right.at[c], dst_ref=from_left.at[c],
            send_sem=send_r.at[c], recv_sem=recv_r.at[c],
            device_id={"replica": lax.rem(here + 1, n_replica)}, device_id_type=mesh_id,
        )

    def leftward(c):
        return pltpu.make_async_remote_copy(
            src_ref=to_left.at[c], dst_ref=from_right.at[c],
            send_sem=send_l.at[c], recv_sem=recv_l.at[c],
            device_id={"replica": lax.rem(here + last, n_replica)}, device_id_type=mesh_id,
        )

    def outward(k):
        return pltpu.make_async_remote_copy(
            src_ref=packed.at[k], dst_ref=pairs.at[k],
            send_sem=send_p.at[k], recv_sem=recv_p.at[k],
            device_id={"expert": flip(index, k, n_expert)}, device_id_type=mesh_id,
        )

    def homeward(k):
        return pltpu.make_async_remote_copy(
            src_ref=back.at[k], dst_ref=ret.at[k],
            send_sem=send_b.at[k], recv_sem=recv_b.at[k],
            device_id={"expert": flip(index, k, n_expert)}, device_id_type=mesh_id,
        )

    barrier = pltpu.get_barrier_semaphore()

    @pl.loop(1, n_expert)
    def _(k):
        pl.semaphore_signal(
            barrier, inc=1, device_id={"expert": flip(index, k, n_expert)}, device_id_type=mesh_id
        )

    @pl.when(here > 0)
    def _():
        pl.semaphore_signal(
            barrier, inc=1, device_id={"replica": lax.rem(here + last, n_replica)},
            device_id_type=mesh_id,
        )

    @pl.when(here < last)
    def _():
        pl.semaphore_signal(
            barrier, inc=1, device_id={"replica": lax.rem(here + 1, n_replica)},
            device_id_type=mesh_id,
        )

    pairs[0] = packed[0]

    @pl.when((here > 0) & (here < last))
    def _():
        pl.semaphore_wait(barrier, n_expert + 1)

    @pl.when((here == 0) | (here == last))
    def _():
        pl.semaphore_wait(barrier, n_expert)

    @pl.loop(1, n_expert)
    def _(k):
        outward(k).start()

    def by_expert(product):
        if per_expert % 16 == 0:
            return jnp.concatenate(
                [product(slice(e * per_expert, (e + 1) * per_expert), e) for e in range(EXP_DEV)],
                axis=0,
            )
        both = [product(slice(0, rows), e) for e in range(EXP_DEV)]
        first = lax.broadcasted_iota(jnp.int32, both[0].shape, 0) < per_expert
        return jnp.where(first, both[0], both[1])

    def first_products(k):
        for w, (side, rhs) in enumerate(((0, a_ref), (0, b_ref), (1, c_ref))):
            part = by_expert(
                lambda at, e: jnp.dot(pairs[k, side, at, :], rhs[e], preferred_element_type=F32)
            )
            own[pl.ds(k * per_source, per_source), :, w * hidden : (w + 1) * hidden] = part.reshape(
                per_source, chunk, hidden
            )

    def slot_gradient(k):
        at_k = pl.ds(k * per_source, per_source)
        gate_part = gate_ref[at_k].reshape(rows, hidden)
        up_part = up_ref[at_k].reshape(rows, hidden)
        dims = (((1,), (1,)), ((), ()))
        return by_expert(
            lambda at, e: lax.dot_general(
                gate_part[at], a_ref[e], dims, preferred_element_type=F32
            )
            + lax.dot_general(up_part[at], b_ref[e], dims, preferred_element_type=F32)
        ).astype(BF)

    @pl.loop(0, n_chunk + HOP_STEPS * last)
    def _(t):
        c_left = t - HOP_STEPS * here
        c_right = t - HOP_STEPS * (last - here)
        done = t - HOP_STEPS * last

        @pl.when((t < n_chunk) & (lax.rem(t, per_source) == 0))
        def _():
            k = t // per_source

            @pl.when(k > 0)
            def _():
                outward(k).wait_recv()

            first_products(k)

        @pl.when((here == 0) & (t < n_chunk))
        def _():
            to_right[t] = own[t].astype(BF)
            rightward(t).start()

        @pl.when((here == last) & (t < n_chunk))
        def _():
            to_left[t] = own[t].astype(BF)
            leftward(t).start()

        @pl.when((here > 0) & (c_left >= 0) & (c_left < n_chunk))
        def _():
            rightward(c_left).wait_recv()

            @pl.when(here < last)
            def _():
                to_right[c_left] = (own[c_left] + from_left[c_left].astype(F32)).astype(BF)
                rightward(c_left).start()

        @pl.when((here < last) & (c_right >= 0) & (c_right < n_chunk))
        def _():
            leftward(c_right).wait_recv()

            @pl.when(here > 0)
            def _():
                to_left[c_right] = (own[c_right] + from_right[c_right].astype(F32)).astype(BF)
                leftward(c_right).start()

        @pl.when(done >= 0)
        def _():
            total[...] = own[done]

            @pl.when(here > 0)
            def _():
                total[...] += from_left[done].astype(F32)

            @pl.when(here < last)
            def _():
                total[...] += from_right[done].astype(F32)

            gate_pre = total[:, :hidden]
            up_pre = total[:, hidden : 2 * hidden]
            hidden_grad = total[:, 2 * hidden :]
            sig = jax.nn.sigmoid(gate_pre)
            silu = gate_pre * sig
            hid_ref[done] = (silu * up_pre).astype(BF)
            up_ref[done] = (hidden_grad * silu).astype(BF)
            gate_ref[done] = (
                hidden_grad * up_pre * sig * (1.0 + gate_pre * (1.0 - sig))
            ).astype(BF)

        @pl.when((done >= 0) & (lax.rem(t - HOP_STEPS * last + per_source, per_source) == per_source - 1))
        def _():
            k = done // per_source

            @pl.when(k == 0)
            def _():
                ret[0] = slot_gradient(0)

            @pl.when(k > 0)
            def _():
                back[k] = slot_gradient(k)
                homeward(k).start()

    @pl.loop(1, n_expert)
    def _(k):
        homeward(k).wait_recv()
        homeward(k).wait_send()
        outward(k).wait_send()

    @pl.loop(0, n_chunk)
    def _(c):
        @pl.when(here < last)
        def _():
            rightward(c).wait_send()

        @pl.when(here > 0)
        def _():
            leftward(c).wait_send()


def middle(n_expert, n_replica, packed, gate_w, up_w, down_w):
    rows, part = packed.shape[2:]
    hidden = gate_w.shape[2]
    chunk = min(32, rows)
    n_chunk = n_expert * rows // chunk
    wide = (n_chunk, chunk, 3 * hidden)
    vmem = pl.BlockSpec(memory_space=pltpu.VMEM)
    one_way = jax.ShapeDtypeStruct((n_expert, rows, part), BF)
    pairs, ret, gate_part, up_part, hid = pl.pallas_call(
        functools.partial(line_kernel, n_expert, n_replica),
        out_shape=[jax.ShapeDtypeStruct(packed.shape, BF), one_way]
        + [jax.ShapeDtypeStruct((n_chunk, chunk, hidden), BF)] * 3,
        in_specs=[vmem] * 4,
        out_specs=[vmem] * 5,
        scratch_shapes=[
            pltpu.VMEM(wide, F32),
            pltpu.VMEM(wide, BF),
            pltpu.VMEM(wide, BF),
            pltpu.VMEM(wide, BF),
            pltpu.VMEM(wide, BF),
            pltpu.VMEM(one_way.shape, BF),
            pltpu.VMEM(wide[1:], F32),
        ]
        + [pltpu.SemaphoreType.DMA((n_chunk,))] * 4
        + [pltpu.SemaphoreType.DMA((n_expert,))] * 4,
        compiler_params=pltpu.CompilerParams(
            collective_id=0, has_side_effects=True, vmem_limit_bytes=56 * 2**20
        ),
        cost_estimate=pl.CostEstimate(
            flops=10 * n_expert * rows * part * hidden,
            bytes_accessed=2**24,
            transcendentals=2**20,
        ),
    )(packed, gate_w, up_w, down_w)
    fold = lambda a: a.reshape(n_expert, EXP_DEV, rows // EXP_DEV, -1)
    term = lambda a, b: jnp.einsum(
        "kerf,kerh->efh", fold(a), fold(b), preferred_element_type=F32
    )
    rows_in, rows_grad = pairs[:, 0], pairs[:, 1]
    return (ret, term(rows_in, gate_part), term(rows_in, up_part), term(rows_grad, hid))


def on_device(x_rows, out_grad, gate_weight, up_weight, down_weight, expert_ids, slot_expert):
    expert_here = lax.axis_index("expert")
    n_expert = lax.axis_size("expert")
    n_replica = lax.axis_size("replica")
    rows, features = x_rows.shape
    part = features // n_replica
    experts_all = EXP_DEV * n_expert
    capacity = max(2, 2 * rows // experts_all)
    own_row = lax.dynamic_index_in_dim(slot_expert, expert_here, 0, keepdims=False)
    local_all = own_row - EXP_DEV * expert_here
    servers = jnp.sum(
        (jnp.arange(EXP_DEV, dtype=jnp.int32)[:, None] == local_all[None, :]).astype(F32), axis=1
    )[:, None, None]

    slot_row = send_slots(expert_ids, experts_all, capacity)
    slot_row = jnp.pad(slot_row.astype(BF), (0, part - rows))
    slot_rows = jnp.broadcast_to(slot_row[None, None, :], (n_replica, 16, part))
    split = lambda a: a.reshape(rows, n_replica, part).transpose(1, 0, 2)
    outgoing = jnp.concatenate([split(x_rows), split(out_grad), slot_rows], axis=1)
    arrived = lax.all_to_all(outgoing, "replica", split_axis=0, concat_axis=0, tiled=True)
    slot_of = arrived[:, 2 * rows, :rows].astype(jnp.int32)
    source = jnp.bitwise_xor(expert_here, jnp.arange(n_expert, dtype=jnp.int32))
    group = EXP_DEV * capacity
    place = (source[:, None] * group + jnp.arange(group, dtype=jnp.int32)[None, :]).reshape(-1)
    pick = (slot_of[:, None, :] == place[None, :, None]).astype(BF)
    pick = pick.reshape(n_replica, n_expert, EXP_DEV, capacity, rows)
    pairs = arrived[:, : 2 * rows].reshape(n_replica, 2, rows, part)
    packed = jnp.einsum("qkecr,qarf->kaeqcf", pick, pairs, preferred_element_type=F32).astype(BF)
    packed = packed.reshape(n_expert, 2, n_replica * group, part)
    back, gate_sum, up_sum, down_sum = middle(
        n_expert, n_replica, packed, gate_weight, up_weight, down_weight
    )
    back = back.reshape(n_expert, EXP_DEV, n_replica, capacity, part)
    x_part = jnp.einsum("qkecr,keqcf->qrf", pick, back, preferred_element_type=F32).astype(BF)
    x_grad = lax.all_to_all(x_part, "replica", split_axis=0, concat_axis=0, tiled=True)
    x_grad = x_grad.transpose(1, 0, 2).reshape(rows, features)
    mean = lambda total: (total / servers).astype(BF)
    return (x_grad, mean(gate_sum), mean(up_sum), mean(down_sum))


def solution(mesh):
    return jax.shard_map(
        on_device,
        mesh=mesh,
        in_specs=(
            P(("expert", "replica"), None),
            P(("expert", "replica"), None),
            P("expert", "replica", None),
            P("expert", "replica", None),
            P("expert", "replica", None),
            P(("expert", "replica")),
            P(),
        ),
        out_specs=(
            P(("expert", "replica"), None),
            P("expert", "replica", None),
            P("expert", "replica", None),
            P("expert", "replica", None),
        ),
        check_vma=False,
    )
```

time: 241 us -> 193 us (0.80)
  blocking collectives: 63.4 us -> 0 us
  waiting for transfers between devices: 17.9 us -> 34.4 us
  Pallas kernels: 121 us -> 129 us
  matrix products: 15.6 us -> 10.8 us
  starting transfers between devices: 13.3 us -> 9.92 us
    all_to_all x2 -> x0, blocking collectives: 63.4 us -> none  [the longest x1 33.2 us: on_device(): lax.all_to_all(outgoing, 'replica', split_axis=0, concat_axis=0, tiled=True)]
    all_to_all x1, waiting for transfers between devices: 11.7 us -> 26.8 us  [on_device(): lax.all_to_all(outgoing, 'replica', split_axis=0, concat_axis=0, tiled=True)]
    pallas_call x1, Pallas kernels: 121 us -> 129 us  [middle(): pl.pallas_call(functools.partial(line_kernel, n_expert, n_replica), out_s...]
    dot_general x7 -> x5, matrix products: 14.7 us -> 9.96 us  [the longest x3 6.63 us: middle(): jnp.einsum('kerf,kerh->efh', fold(a), fold(b), preferred_element_type=F32)]
    all_to_all x1, starting transfers between devices: 9.82 us -> 6.45 us  [on_device(): lax.all_to_all(outgoing, 'replica', split_axis=0, concat_axis=0, tiled=True)]
where the time goes in v3:
time: 193 us
  Pallas kernels  129 us (67%)
  waiting for transfers between devices  34.4 us (18%)
  matrix products  10.8 us (6%)
  starting transfers between devices  9.92 us (5%)
  local copies, waits for them, and re-layouts  5.63 us (3%)
  other arithmetic  2.16 us (1%)
    pallas_call x1, Pallas kernels, middle(): pl.pallas_call(functools.partial(line_kernel, n_expert, n_replica), out_s...  129 us
    all_to_all x1, waiting for transfers between devices, on_device(): lax.all_to_all(outgoing, 'replica', split_axis=0, concat_axis=0, tiled=True)  26.8 us
    all_to_all x1, waiting for transfers between devices, on_device(): lax.all_to_all(x_part, 'replica', split_axis=0, concat_axis=0, tiled=True)  7.62 us
    dot_general x3, matrix products, middle(): jnp.einsum('kerf,kerh->efh', fold(a), fold(b), preferred_element_type=F32)  6.63 us
    all_to_all x1, starting transfers between devices, on_device(): lax.all_to_all(outgoing, 'replica', split_axis=0, concat_axis=0, tiled=True)  6.45 us
  transfers between devices with their start and end apart: 2, of which 2 were waited for; matrix products, arithmetic and copies ran while one was open for 4% of the time, Pallas kernels for 0%

profile of v3, /device:TPU:0, one launch (start us, length us, event | category | flops | bytes accessed | tf_op | source)
XLA Modules:
  0.0 192.7 jit_solution(9289492373083717935)
XLA Ops:
  0.6 0.9 fusion.4
  1.5 0.7 add_convert_fusion
  2.2 1.3 bitcast_bitcast_fusion
  3.5 1.1 pad_maximum_fusion
  4.6 0.0 copy-start.1
  4.6 6.4 %all-to-all-start = ((bf16[4,272,512]{2,1,0:T(8,128)(2,1)}), bf16[4,272,512]{2,1,0:T(8,128)(2,1)S(1)}, u32[]{:S(2)}, u32[]{:S(2)}) async-start(bf16[4,272,512]{2,1,0:T(8,128)(2,1)} %pad_maximum_fusion), calls=%async_computation | async-start | bytes 2228224 | tf_op jit(solution)/shard_map/all_to_all | solution.py:306
  11.1 0.0 copy-done.1
  11.1 0.2 subtract_reduce_fusion
  11.3 0.1 fusion.12
  11.4 0.1 add_add_fusion
  11.4 26.8 %all-to-all-done = bf16[4,272,512]{2,1,0:T(8,128)(2,1)S(1)} async-done(((bf16[4,272,512]{2,1,0:T(8,128)(2,1)}), bf16[4,272,512]{2,1,0:T(8,128)(2,1)S(1)}, u32[]{:S(2)}, u32[]{:S(2)}) %all-to-all-start) | async-done | bytes 1114144 | tf_op jit(solution)/shard_map/all_to_all | solution.py:306
  38.2 0.1 slice.17
  38.3 0.7 convert_bitcast_fusion
  39.0 1.5 copy.38
  40.6 129.0 %shard_map.102 = (bf16[8,2,128,512]{3,2,1,0:T(8,128)(2,1)}, bf16[8,128,512]{2,1,0:T(8,128)(2,1)}, bf16[32,32,768]{2,1,0:T(8,128)(2,1)}, bf16[32,32,768]{2,1,0:T(8,128)(2,1)}, bf16[32,32,768]{2,1,0:T(8,128)(2,1)}) custom-call(bf16[8,2,128,512]{3,2,1,0:T(8,128)(2,1)} %bitcast.56, bf16[2,512,768]{2,1,0:T(8,128)(2,1)} %a_ref.1, bf16[2,512,768]{2,1,0:T(8,128)(2,1)} %b_ref.1, ...), custom_call_target="tpu_custom_call" | custom-call | flops 4026531840 | bytes 16777216 | tf_op jit(solution)/shard_map/pallas_call | solution.py:253
  169.7 0.0 copy-start
  169.7 2.6 %fusion.3 = bf16[4,128,512]{2,1,0:T(8,128)(2,1)} fusion(bf16[8,2,4,16,512]{4,3,2,1,0:T(8,128)(2,1)} %bitcast.70, s32[8,2,16]{2,0,1:T(8,128)S(1)} %add_add_fusion, s32[4,128]{1,0:T(4,128)S(1)} %bitcast.66), kind=kOutput, calls=%fused_computation.8 | convolution fusion | flops 134610944 | bytes 1575936 | tf_op jit(solution)/shard_map/qkecr,keqcf->qrf/dot_general | solution.py:320
  172.2 3.5 %all-to-all-start.1 = ((bf16[4,128,512]{2,1,0:T(8,128)(2,1)}), bf16[4,128,512]{2,1,0:T(8,128)(2,1)S(1)}, u32[]{:S(2)}, u32[]{:S(2)}) async-start(bf16[4,128,512]{2,1,0:T(8,128)(2,1)} %fusion.3), calls=%async_computation.1 | async-start | bytes 1048576 | tf_op jit(solution)/shard_map/all_to_all | solution.py:321
  175.7 0.0 copy-done
  175.7 0.0 copy-start.4
  175.7 0.2 fusion.13
  176.0 1.2 copy-done.4
  177.1 0.0 copy-start.3
  177.1 2.2 %fusion.1 = bf16[2,512,768]{2,1,0:T(8,128)(2,1)} fusion(bf16[8,2,64,512]{3,2,1,0:T(8,128)(2,1)S(1)} %bitcast.61, bf16[8,2,64,768]{3,2,1,0:T(8,128)(2,1)S(1)} %bitcast.69, f32[2]{0:T(128)S(1)} %fusion.12), kind=kOutput, calls=%fused_computation.3 | convolution fusion | flops 806879232 | bytes 4194312 | tf_op jit(solution)/shard_map/kerf,kerh->efh/dot_general | solution.py:280
  179.4 0.0 copy-done.3
  179.4 0.0 copy-start.2
  179.4 2.2 %fusion.2 = bf16[2,512,768]{2,1,0:T(8,128)(2,1)} fusion(bf16[8,2,64,512]{3,2,1,0:T(8,128)(2,1)S(1)} %bitcast.62, bf16[8,2,64,768]{3,2,1,0:T(8,128)(2,1)S(1)} %bitcast.68, f32[2]{0:T(128)S(1)} %fusion.12), kind=kOutput, calls=%fused_computation.5 | convolution fusion | flops 806879232 | bytes 4194312 | tf_op jit(solution)/shard_map/kerf,kerh->efh/dot_general | solution.py:280
  181.6 0.0 copy-done.2
  181.6 2.2 %fusion = bf16[2,512,768]{2,1,0:T(8,128)(2,1)} fusion(bf16[8,2,64,512]{3,2,1,0:T(8,128)(2,1)S(1)} %bitcast.60, bf16[8,2,64,768]{3,2,1,0:T(8,128)(2,1)S(1)} %bitcast.67, f32[2]{0:T(128)S(1)} %fusion.12), kind=kOutput, calls=%fused_computation.1 | convolution fusion | flops 806879232 | bytes 4194312 | tf_op jit(solution)/shard_map/kerf,kerh->efh/dot_general | solution.py:280
  183.8 7.6 %all-to-all-done.1 = bf16[4,128,512]{2,1,0:T(8,128)(2,1)S(1)} async-done(((bf16[4,128,512]{2,1,0:T(8,128)(2,1)}), bf16[4,128,512]{2,1,0:T(8,128)(2,1)S(1)}, u32[]{:S(2)}, u32[]{:S(2)}) %all-to-all-start.1) | async-done | bytes 524320 | tf_op jit(solution)/shard_map/all_to_all | solution.py:321
  191.4 0.3 copy.40
  191.7 1.0 copy.41
  (4 shorter events, 0.0 us)
Async XLA Ops:
  4.6 6.5 %copy-start.1 = (s32[8,4]{0,1:T(4,128)S(1)}, s32[8,4]{0,1:T(4,128)}, u32[]{:S(2)}) copy-start(s32[8,4]{0,1:T(4,128)} %param.13) | copy-start | bytes 388
  4.6 33.6 %all-to-all-start = ((bf16[4,272,512]{2,1,0:T(8,128)(2,1)}), bf16[4,272,512]{2,1,0:T(8,128)(2,1)S(1)}, u32[]{:S(2)}, u32[]{:S(2)}) async-start(bf16[4,272,512]{2,1,0:T(8,128)(2,1)} %pad_maximum_fusion), calls=%async_computation | async-start | bytes 2228224 | tf_op jit(solution)/shard_map/all_to_all | solution.py:306
  169.7 6.1 %copy-start = (bf16[8,2,128,512]{3,2,1,0:T(8,128)(2,1)S(1)}, bf16[8,2,128,512]{3,2,1,0:T(8,128)(2,1)}, u32[]{:S(2)}) copy-start(bf16[8,2,128,512]{3,2,1,0:T(8,128)(2,1)} %get-tuple-element.10) | copy-start | bytes 6291460
  172.2 19.2 %all-to-all-start.1 = ((bf16[4,128,512]{2,1,0:T(8,128)(2,1)}), bf16[4,128,512]{2,1,0:T(8,128)(2,1)S(1)}, u32[]{:S(2)}, u32[]{:S(2)}) async-start(bf16[4,128,512]{2,1,0:T(8,128)(2,1)} %fusion.3), calls=%async_computation.1 | async-start | bytes 1048576 | tf_op jit(solution)/shard_map/all_to_all | solution.py:321
  175.7 1.4 copy-start.4
  177.1 2.2 %copy-start.3 = (bf16[32,32,768]{2,1,0:T(8,128)(2,1)S(1)}, bf16[32,32,768]{2,1,0:T(8,128)(2,1)}, u32[]{:S(2)}) copy-start(bf16[32,32,768]{2,1,0:T(8,128)(2,1)} %get-tuple-element.11) | copy-start | bytes 4718596
  179.4 2.2 %copy-start.2 = (bf16[32,32,768]{2,1,0:T(8,128)(2,1)S(1)}, bf16[32,32,768]{2,1,0:T(8,128)(2,1)}, u32[]{:S(2)}) copy-start(bf16[32,32,768]{2,1,0:T(8,128)(2,1)} %get-tuple-element.13) | copy-start | bytes 4718596

commit v4 on v3

--- a/solution.py
+++ b/solution.py
@@ -36,18 +36,23 @@
 
 
 def line_kernel(
-    n_expert, n_replica, packed, a_ref, b_ref, c_ref, pairs, ret, gate_ref, up_ref, hid_ref,
-    own, from_left, from_right, to_right, to_left, back, total,
-    send_r, recv_r, send_l, recv_l, send_p, recv_p, send_b, recv_b,
+    n_expert, n_replica, x_ref, g_ref, slot_ref, a_ref, b_ref, c_ref,
+    pairs, ret, gate_ref, up_ref, hid_ref, slots_in,
+    x_in, g_in, packed, own, from_left, from_right, to_right, to_left, back, total,
+    send_r, recv_r, send_l, recv_l, send_p, recv_p, send_b, recv_b, send_z, recv_z,
 ):
     here = lax.axis_index("replica")
     index = lax.axis_index("expert")
     last = n_replica - 1
     n_chunk, chunk, _ = own.shape
     hidden = a_ref.shape[2]
-    rows = packed.shape[2]
+    rows = pairs.shape[2]
     per_source = rows // chunk
     per_expert = rows // EXP_DEV
+    held = x_ref.shape[0]
+    part = x_in.shape[1]
+    group = rows // n_replica
+    capacity = group // EXP_DEV
     mesh_id = pl.DeviceIdType.MESH
 
     def rightward(c):
@@ -78,6 +83,35 @@
             device_id={"expert": flip(index, k, n_expert)}, device_id_type=mesh_id,
         )
 
+    def quarters(q):
+        columns = pl.ds(pl.multiple_of(q * part, part), part)
+        at = pl.ds(pl.multiple_of(here * held, held), held)
+        return (
+            (x_ref.at[:, columns], x_in.at[at]),
+            (g_ref.at[:, columns], g_in.at[at]),
+            (slot_ref, slots_in.at[here]),
+        )
+
+    def across(q):
+        return [
+            pltpu.make_async_remote_copy(
+                src_ref=src, dst_ref=dst, send_sem=send_z.at[w, q], recv_sem=recv_z.at[w, here],
+                device_id={"replica": q}, device_id_type=mesh_id,
+            )
+            for w, (src, dst) in enumerate(quarters(q))
+        ]
+
+    def arriving(q):
+        at = pl.ds(pl.multiple_of(q * held, held), held)
+        landed = (x_in.at[at], g_in.at[at], slots_in.at[q])
+        return [
+            pltpu.make_async_remote_copy(
+                src_ref=dst, dst_ref=dst, send_sem=send_z.at[w, q], recv_sem=recv_z.at[w, q],
+                device_id={"replica": q}, device_id_type=mesh_id,
+            )
+            for w, dst in enumerate(landed)
+        ]
+
     barrier = pltpu.get_barrier_semaphore()
 
     @pl.loop(1, n_expert)
@@ -86,32 +120,60 @@
             barrier, inc=1, device_id={"expert": flip(index, k, n_expert)}, device_id_type=mesh_id
         )
 
-    @pl.when(here > 0)
-    def _():
+    @pl.loop(1, n_replica)
+    def _(k):
         pl.semaphore_signal(
-            barrier, inc=1, device_id={"replica": lax.rem(here + last, n_replica)},
+            barrier, inc=1, device_id={"replica": lax.rem(here + k, n_replica)},
             device_id_type=mesh_id,
         )
 
-    @pl.when(here < last)
-    def _():
-        pl.semaphore_signal(
-            barrier, inc=1, device_id={"replica": lax.rem(here + 1, n_replica)},
-            device_id_type=mesh_id,
-        )
-
-    pairs[0] = packed[0]
-
-    @pl.when((here > 0) & (here < last))
-    def _():
-        pl.semaphore_wait(barrier, n_expert + 1)
-
-    @pl.when((here == 0) | (here == last))
-    def _():
-        pl.semaphore_wait(barrier, n_expert)
+    pl.semaphore_wait(barrier, n_expert + n_replica - 2)
+
+    @pl.loop(1, n_replica)
+    def _(k):
+        for copy in across(lax.rem(here + k, n_replica)):
+            copy.start()
+
+    mine = [
+        pltpu.make_async_copy(src, dst, send_z.at[w, here])
+        for w, (src, dst) in enumerate(quarters(here))
+    ]
+    for copy in mine:
+        copy.start()
+    for copy in mine:
+        copy.wait()
+
+    @pl.loop(1, n_replica)
+    def _(k):
+        for copy in arriving(lax.rem(here + k, n_replica)):
+            copy.wait_recv()
+
+    span = n_expert * group
+    keys = jnp.concatenate(
+        [slots_in[q, 0:1, :].astype(F32) + float(q * span) for q in range(n_replica)], axis=1
+    ).astype(jnp.int32)
+
+    def pack(k):
+        row = lax.broadcasted_iota(jnp.int32, (rows, 1), 0)
+        local = row // per_expert
+        sender = (row // capacity) % n_replica
+        want = (
+            sender * span
+            + flip(index, k, n_expert) * group
+            + local * capacity
+            + row % capacity
+        )
+        pick = jnp.where(want == keys, 1.0, 0.0).astype(BF)
+        return [
+            jnp.dot(pick, side[...], preferred_element_type=F32).astype(BF)
+            for side in (x_in, g_in)
+        ]
+
+    pairs[0, 0], pairs[0, 1] = pack(0)
 
     @pl.loop(1, n_expert)
     def _(k):
+        packed[k, 0], packed[k, 1] = pack(k)
         outward(k).start()
 
     def by_expert(product):
@@ -231,6 +293,11 @@
         homeward(k).wait_send()
         outward(k).wait_send()
 
+    @pl.loop(1, n_replica)
+    def _(k):
+        for copy in across(lax.rem(here + k, n_replica)):
+            copy.wait_send()
+
     @pl.loop(0, n_chunk)
     def _(c):
         @pl.when(here < last)
@@ -242,21 +309,27 @@
             leftward(c).wait_send()
 
 
-def middle(n_expert, n_replica, packed, gate_w, up_w, down_w):
-    rows, part = packed.shape[2:]
+def middle(n_expert, n_replica, capacity, x_rows, out_grad, slot_rows, gate_w, up_w, down_w):
+    rows, part = EXP_DEV * n_replica * capacity, gate_w.shape[1]
+    held = x_rows.shape[0]
+    both = (n_expert, 2, rows, part)
     hidden = gate_w.shape[2]
     chunk = min(32, rows)
     n_chunk = n_expert * rows // chunk
     wide = (n_chunk, chunk, 3 * hidden)
     vmem = pl.BlockSpec(memory_space=pltpu.VMEM)
     one_way = jax.ShapeDtypeStruct((n_expert, rows, part), BF)
-    pairs, ret, gate_part, up_part, hid = pl.pallas_call(
+    pairs, ret, gate_part, up_part, hid, slots_in = pl.pallas_call(
         functools.partial(line_kernel, n_expert, n_replica),
-        out_shape=[jax.ShapeDtypeStruct(packed.shape, BF), one_way]
-        + [jax.ShapeDtypeStruct((n_chunk, chunk, hidden), BF)] * 3,
-        in_specs=[vmem] * 4,
-        out_specs=[vmem] * 5,
+        out_shape=[jax.ShapeDtypeStruct(both, BF), one_way]
+        + [jax.ShapeDtypeStruct((n_chunk, chunk, hidden), BF)] * 3
+        + [jax.ShapeDtypeStruct((n_replica,) + slot_rows.shape, BF)],
+        in_specs=[vmem] * 6,
+        out_specs=[vmem] * 6,
         scratch_shapes=[
+            pltpu.VMEM((n_replica * held, part), BF),
+            pltpu.VMEM((n_replica * held, part), BF),
+            pltpu.VMEM(both, BF),
             pltpu.VMEM(wide, F32),
             pltpu.VMEM(wide, BF),
             pltpu.VMEM(wide, BF),
@@ -266,7 +339,8 @@
             pltpu.VMEM(wide[1:], F32),
         ]
         + [pltpu.SemaphoreType.DMA((n_chunk,))] * 4
-        + [pltpu.SemaphoreType.DMA((n_expert,))] * 4,
+        + [pltpu.SemaphoreType.DMA((n_expert,))] * 4
+        + [pltpu.SemaphoreType.DMA((3, n_replica))] * 2,
         compiler_params=pltpu.CompilerParams(
             collective_id=0, has_side_effects=True, vmem_limit_bytes=56 * 2**20
         ),
@@ -275,13 +349,13 @@
             bytes_accessed=2**24,
             transcendentals=2**20,
         ),
-    )(packed, gate_w, up_w, down_w)
+    )(x_rows, out_grad, slot_rows, gate_w, up_w, down_w)
     fold = lambda a: a.reshape(n_expert, EXP_DEV, rows // EXP_DEV, -1)
     term = lambda a, b: jnp.einsum(
         "kerf,kerh->efh", fold(a), fold(b), preferred_element_type=F32
     )
     rows_in, rows_grad = pairs[:, 0], pairs[:, 1]
-    return (ret, term(rows_in, gate_part), term(rows_in, up_part), term(rows_grad, hid))
+    return (ret, slots_in, term(rows_in, gate_part), term(rows_in, up_part), term(rows_grad, hid))
 
 
 def on_device(x_rows, out_grad, gate_weight, up_weight, down_weight, expert_ids, slot_expert):
@@ -299,23 +373,17 @@
     )[:, None, None]
 
     slot_row = send_slots(expert_ids, experts_all, capacity)
-    slot_row = jnp.pad(slot_row.astype(BF), (0, part - rows))
-    slot_rows = jnp.broadcast_to(slot_row[None, None, :], (n_replica, 16, part))
-    split = lambda a: a.reshape(rows, n_replica, part).transpose(1, 0, 2)
-    outgoing = jnp.concatenate([split(x_rows), split(out_grad), slot_rows], axis=1)
-    arrived = lax.all_to_all(outgoing, "replica", split_axis=0, concat_axis=0, tiled=True)
-    slot_of = arrived[:, 2 * rows, :rows].astype(jnp.int32)
+    slot_rows = jnp.broadcast_to(slot_row.astype(BF)[None, :], (16, rows))
+    back, slots_in, gate_sum, up_sum, down_sum = middle(
+        n_expert, n_replica, capacity, x_rows, out_grad, slot_rows,
+        gate_weight, up_weight, down_weight,
+    )
+    slot_of = slots_in[:, 0, :].astype(jnp.int32)
     source = jnp.bitwise_xor(expert_here, jnp.arange(n_expert, dtype=jnp.int32))
     group = EXP_DEV * capacity
     place = (source[:, None] * group + jnp.arange(group, dtype=jnp.int32)[None, :]).reshape(-1)
     pick = (slot_of[:, None, :] == place[None, :, None]).astype(BF)
     pick = pick.reshape(n_replica, n_expert, EXP_DEV, capacity, rows)
-    pairs = arrived[:, : 2 * rows].reshape(n_replica, 2, rows, part)
-    packed = jnp.einsum("qkecr,qarf->kaeqcf", pick, pairs, preferred_element_type=F32).astype(BF)
-    packed = packed.reshape(n_expert, 2, n_replica * group, part)
-    back, gate_sum, up_sum, down_sum = middle(
-        n_expert, n_replica, packed, gate_weight, up_weight, down_weight
-    )
     back = back.reshape(n_expert, EXP_DEV, n_replica, capacity, part)
     x_part = jnp.einsum("qkecr,keqcf->qrf", pick, back, preferred_element_type=F32).astype(BF)
     x_grad = lax.all_to_all(x_part, "replica", split_axis=0, concat_axis=0, tiled=True)

time: 193 us -> 184 us (0.953)
  Pallas kernels: 129 us -> 158 us
  waiting for transfers between devices: 34.4 us -> 6.97 us
  starting transfers between devices: 9.92 us -> 3.47 us
  local copies, waits for them, and re-layouts: 5.63 us -> 3.29 us
    pallas_call x1, Pallas kernels: 129 us -> 158 us  [middle(): pl.pallas_call(functools.partial(line_kernel, n_expert, n_replica), out_s...]
    all_to_all x1 -> x0, waiting for transfers between devices: 26.8 us -> none  [on_device(): lax.all_to_all(outgoing, 'replica', split_axis=0, concat_axis=0, tiled=True)]
    all_to_all x1 -> x0, starting transfers between devices: 6.45 us -> none  [on_device(): lax.all_to_all(outgoing, 'replica', split_axis=0, concat_axis=0, tiled=True)]
  transfers between devices with their start and end apart: 2 -> 1, of which waited for: 2 -> 1; matrix products, arithmetic and copies ran while one was open for 4% -> 4% of each run, Pallas kernels for 0% -> 0%
where the time goes in v4:
time: 184 us
  Pallas kernels  158 us (86%)
  matrix products  9.94 us (5%)
  waiting for transfers between devices  6.97 us (4%)
  starting transfers between devices  3.47 us (2%)
  local copies, waits for them, and re-layouts  3.29 us (2%)
  other arithmetic  1.91 us (1%)
    pallas_call x1, Pallas kernels, middle(): pl.pallas_call(functools.partial(line_kernel, n_expert, n_replica), out_s...  158 us
    all_to_all x1, waiting for transfers between devices, on_device(): lax.all_to_all(x_part, 'replica', split_axis=0, concat_axis=0, tiled=True)  6.97 us
    dot_general x3, matrix products, middle(): jnp.einsum('kerf,kerh->efh', fold(a), fold(b), preferred_element_type=F32)  6.62 us
  transfers between devices with their start and end apart: 1, of which 1 were waited for; matrix products, arithmetic and copies ran while one was open for 4% of the time, Pallas kernels for 0%

profile of v4, /device:TPU:0, one launch (start us, length us, event | category | flops | bytes accessed | tf_op | source)
XLA Modules:
  0.0 184.1 jit_solution(14153208112366975491)
XLA Ops:
  0.6 0.9 fusion.4
  1.5 0.7 add_convert_fusion
  2.2 0.1 add_add_fusion
  2.3 0.6 broadcast_in_dim.2.slot_ref
  2.9 157.8 %shard_map.102 = (bf16[8,2,128,512]{3,2,1,0:T(8,128)(2,1)}, bf16[8,128,512]{2,1,0:T(8,128)(2,1)}, bf16[32,32,768]{2,1,0:T(8,128)(2,1)}, bf16[32,32,768]{2,1,0:T(...) custom-call(bf16[128,2048]{1,0:T(8,128)(2,1)} %x_ref.1, bf16[128,2048]{1,0:T(8,128)(2,1)} %g_ref.1, ...), custom_call_target="tpu_custom_call" | custom-call | flops 4026531840 | bytes 16777216 | tf_op jit(solution)/shard_map/pallas_call | solution.py:322
  160.6 0.0 copy-start.1
  160.7 0.0 copy-start
  160.7 0.9 slice_convert_fusion
  161.5 2.4 %fusion.3 = bf16[4,128,512]{2,1,0:T(8,128)(2,1)} fusion(bf16[8,2,4,16,512]{4,3,2,1,0:T(8,128)(2,1)} %bitcast.42, s32[8,2,16]{2,0,1:T(8,128)S(1)} %add_add_fusion, s32[4,128]{1,0:T(4,128)S(1)} %bitcast.38), kind=kOutput, calls=%fused_computation.7 | convolution fusion | flops 134610944 | bytes 1575936 | tf_op jit(solution)/shard_map/qkecr,keqcf->qrf/dot_general | solution.py:388
  164.0 3.5 %all-to-all-start = ((bf16[4,128,512]{2,1,0:T(8,128)(2,1)}), bf16[4,128,512]{2,1,0:T(8,128)(2,1)S(1)}, u32[]{:S(2)}, u32[]{:S(2)}) async-start(bf16[4,128,512]{2,1,0:T(8,128)(2,1)} %fusion.3), calls=%async_computation | async-start | bytes 1048576 | tf_op jit(solution)/shard_map/all_to_all | solution.py:389
  167.4 0.0 copy-done.1
  167.4 0.2 subtract_reduce_fusion
  167.6 0.1 fusion.11
  167.8 0.0 copy-done
  167.8 0.0 copy-start.4
  167.8 0.2 fusion.12
  168.0 1.2 copy-done.4
  169.2 0.0 copy-start.3
  169.2 2.2 %fusion.1 = bf16[2,512,768]{2,1,0:T(8,128)(2,1)} fusion(bf16[8,2,64,512]{3,2,1,0:T(8,128)(2,1)S(1)} %bitcast.36, bf16[8,2,64,768]{3,2,1,0:T(8,128)(2,1)S(1)} %bitcast.41, f32[2]{0:T(128)S(1)} %fusion.11), kind=kOutput, calls=%fused_computation.3 | convolution fusion | flops 806879232 | bytes 4194312 | tf_op jit(solution)/shard_map/kerf,kerh->efh/dot_general | solution.py:354
  171.4 0.0 copy-done.3
  171.4 0.0 copy-start.2
  171.4 2.2 %fusion.2 = bf16[2,512,768]{2,1,0:T(8,128)(2,1)} fusion(bf16[8,2,64,512]{3,2,1,0:T(8,128)(2,1)S(1)} %bitcast.37, bf16[8,2,64,768]{3,2,1,0:T(8,128)(2,1)S(1)} %bitcast.40, f32[2]{0:T(128)S(1)} %fusion.11), kind=kOutput, calls=%fused_computation.5 | convolution fusion | flops 806879232 | bytes 4194312 | tf_op jit(solution)/shard_map/kerf,kerh->efh/dot_general | solution.py:354
  173.6 0.0 copy-done.2
  173.6 2.2 %fusion = bf16[2,512,768]{2,1,0:T(8,128)(2,1)} fusion(bf16[8,2,64,512]{3,2,1,0:T(8,128)(2,1)S(1)} %bitcast.35, bf16[8,2,64,768]{3,2,1,0:T(8,128)(2,1)S(1)} %bitcast.39, f32[2]{0:T(128)S(1)} %fusion.11), kind=kOutput, calls=%fused_computation.1 | convolution fusion | flops 806879232 | bytes 4194312 | tf_op jit(solution)/shard_map/kerf,kerh->efh/dot_general | solution.py:354
  175.8 7.0 %all-to-all-done = bf16[4,128,512]{2,1,0:T(8,128)(2,1)S(1)} async-done(((bf16[4,128,512]{2,1,0:T(8,128)(2,1)}), bf16[4,128,512]{2,1,0:T(8,128)(2,1)S(1)}, u32[]{:S(2)}, u32[]{:S(2)}) %all-to-all-start) | async-done | bytes 524320 | tf_op jit(solution)/shard_map/all_to_all | solution.py:389
  182.8 0.3 copy.28
  183.0 1.0 copy.29
  (1 shorter events, 0.0 us)
Async XLA Ops:
  160.6 6.8 %copy-start.1 = (s32[8,4]{0,1:T(4,128)S(1)}, s32[8,4]{0,1:T(4,128)}, u32[]{:S(2)}) copy-start(s32[8,4]{0,1:T(4,128)} %param.13) | copy-start | bytes 388
  160.7 7.1 %copy-start = (bf16[8,2,128,512]{3,2,1,0:T(8,128)(2,1)S(1)}, bf16[8,2,128,512]{3,2,1,0:T(8,128)(2,1)}, u32[]{:S(2)}) copy-start(bf16[8,2,128,512]{3,2,1,0:T(8,128)(2,1)} %get-tuple-element.12) | copy-start | bytes 6291460
  164.0 18.8 %all-to-all-start = ((bf16[4,128,512]{2,1,0:T(8,128)(2,1)}), bf16[4,128,512]{2,1,0:T(8,128)(2,1)S(1)}, u32[]{:S(2)}, u32[]{:S(2)}) async-start(bf16[4,128,512]{2,1,0:T(8,128)(2,1)} %fusion.3), calls=%async_computation | async-start | bytes 1048576 | tf_op jit(solution)/shard_map/all_to_all | solution.py:389
  167.8 1.4 copy-start.4
  169.2 2.2 %copy-start.3 = (bf16[32,32,768]{2,1,0:T(8,128)(2,1)S(1)}, bf16[32,32,768]{2,1,0:T(8,128)(2,1)}, u32[]{:S(2)}) copy-start(bf16[32,32,768]{2,1,0:T(8,128)(2,1)} %get-tuple-element.13) | copy-start | bytes 4718596
  171.4 2.2 %copy-start.2 = (bf16[32,32,768]{2,1,0:T(8,128)(2,1)S(1)}, bf16[32,32,768]{2,1,0:T(8,128)(2,1)}, u32[]{:S(2)}) copy-start(bf16[32,32,768]{2,1,0:T(8,128)(2,1)} %get-tuple-element.15) | copy-start | bytes 4718596

commit v5 on v4

--- a/solution.py
+++ b/solution.py
@@ -171,11 +171,6 @@
 
     pairs[0, 0], pairs[0, 1] = pack(0)
 
-    @pl.loop(1, n_expert)
-    def _(k):
-        packed[k, 0], packed[k, 1] = pack(k)
-        outward(k).start()
-
     def by_expert(product):
         if per_expert % 16 == 0:
             return jnp.concatenate(
@@ -232,6 +227,12 @@
         def _():
             to_left[t] = own[t].astype(BF)
             leftward(t).start()
+
+        @pl.when(t < n_expert - 1)
+        def _():
+            k = t + 1
+            packed[k, 0], packed[k, 1] = pack(k)
+            outward(k).start()
 
         @pl.when((here > 0) & (c_left >= 0) & (c_left < n_chunk))
         def _():

time: 184 us -> 182 us (0.989)
  Pallas kernels: 158 us -> 156 us
    pallas_call x1, Pallas kernels: 158 us -> 156 us  [middle(): pl.pallas_call(functools.partial(line_kernel, n_expert, n_replica), out_s...]
where the time goes in v5:
time: 182 us
  Pallas kernels  156 us (86%)
  matrix products  9.94 us (5%)
  waiting for transfers between devices  6.98 us (4%)
  starting transfers between devices  3.47 us (2%)
  local copies, waits for them, and re-layouts  3.29 us (2%)
  other arithmetic  1.91 us (1%)
    pallas_call x1, Pallas kernels, middle(): pl.pallas_call(functools.partial(line_kernel, n_expert, n_replica), out_s...  156 us
    all_to_all x1, waiting for transfers between devices, on_device(): lax.all_to_all(x_part, 'replica', split_axis=0, concat_axis=0, tiled=True)  6.98 us
    dot_general x3, matrix products, middle(): jnp.einsum('kerf,kerh->efh', fold(a), fold(b), preferred_element_type=F32)  6.62 us
  transfers between devices with their start and end apart: 1, of which 1 were waited for; matrix products, arithmetic and copies ran while one was open for 4% of the time, Pallas kernels for 0%

profile of v5, /device:TPU:0, one launch (start us, length us, event | category | flops | bytes accessed | tf_op | source)
XLA Modules:
  0.0 181.9 jit_solution(18336007268831827331)
XLA Ops:
  0.6 0.9 fusion.4
  1.5 0.7 add_convert_fusion
  2.2 0.1 add_add_fusion
  2.3 0.6 broadcast_in_dim.2.slot_ref
  2.9 155.6 %shard_map.102 = (bf16[8,2,128,512]{3,2,1,0:T(8,128)(2,1)}, bf16[8,128,512]{2,1,0:T(8,128)(2,1)}, bf16[32,32,768]{2,1,0:T(8,128)(2,1)}, bf16[32,32,768]{2,1,0:T(...) custom-call(bf16[128,2048]{1,0:T(8,128)(2,1)} %x_ref.1, bf16[128,2048]{1,0:T(8,128)(2,1)} %g_ref.1, ...), custom_call_target="tpu_custom_call" | custom-call | flops 4026531840 | bytes 16777216 | tf_op jit(solution)/shard_map/pallas_call | solution.py:323
  158.5 0.0 copy-start.1
  158.5 0.0 copy-start
  158.5 0.9 slice_convert_fusion
  159.3 2.4 %fusion.3 = bf16[4,128,512]{2,1,0:T(8,128)(2,1)} fusion(bf16[8,2,4,16,512]{4,3,2,1,0:T(8,128)(2,1)} %bitcast.42, s32[8,2,16]{2,0,1:T(8,128)S(1)} %add_add_fusion, s32[4,128]{1,0:T(4,128)S(1)} %bitcast.38), kind=kOutput, calls=%fused_computation.7 | convolution fusion | flops 134610944 | bytes 1575936 | tf_op jit(solution)/shard_map/qkecr,keqcf->qrf/dot_general | solution.py:389
  161.8 3.5 %all-to-all-start = ((bf16[4,128,512]{2,1,0:T(8,128)(2,1)}), bf16[4,128,512]{2,1,0:T(8,128)(2,1)S(1)}, u32[]{:S(2)}, u32[]{:S(2)}) async-start(bf16[4,128,512]{2,1,0:T(8,128)(2,1)} %fusion.3), calls=%async_computation | async-start | bytes 1048576 | tf_op jit(solution)/shard_map/all_to_all | solution.py:390
  165.3 0.0 copy-done.1
  165.3 0.2 subtract_reduce_fusion
  165.5 0.1 fusion.11
  165.6 0.0 copy-done
  165.6 0.0 copy-start.4
  165.6 0.2 fusion.12
  165.8 1.2 copy-done.4
  167.0 0.0 copy-start.3
  167.0 2.2 %fusion.1 = bf16[2,512,768]{2,1,0:T(8,128)(2,1)} fusion(bf16[8,2,64,512]{3,2,1,0:T(8,128)(2,1)S(1)} %bitcast.36, bf16[8,2,64,768]{3,2,1,0:T(8,128)(2,1)S(1)} %bitcast.41, f32[2]{0:T(128)S(1)} %fusion.11), kind=kOutput, calls=%fused_computation.3 | convolution fusion | flops 806879232 | bytes 4194312 | tf_op jit(solution)/shard_map/kerf,kerh->efh/dot_general | solution.py:355
  169.2 0.0 copy-done.3
  169.2 0.0 copy-start.2
  169.2 2.2 %fusion.2 = bf16[2,512,768]{2,1,0:T(8,128)(2,1)} fusion(bf16[8,2,64,512]{3,2,1,0:T(8,128)(2,1)S(1)} %bitcast.37, bf16[8,2,64,768]{3,2,1,0:T(8,128)(2,1)S(1)} %bitcast.40, f32[2]{0:T(128)S(1)} %fusion.11), kind=kOutput, calls=%fused_computation.5 | convolution fusion | flops 806879232 | bytes 4194312 | tf_op jit(solution)/shard_map/kerf,kerh->efh/dot_general | solution.py:355
  171.4 0.0 copy-done.2
  171.4 2.2 %fusion = bf16[2,512,768]{2,1,0:T(8,128)(2,1)} fusion(bf16[8,2,64,512]{3,2,1,0:T(8,128)(2,1)S(1)} %bitcast.35, bf16[8,2,64,768]{3,2,1,0:T(8,128)(2,1)S(1)} %bitcast.39, f32[2]{0:T(128)S(1)} %fusion.11), kind=kOutput, calls=%fused_computation.1 | convolution fusion | flops 806879232 | bytes 4194312 | tf_op jit(solution)/shard_map/kerf,kerh->efh/dot_general | solution.py:355
  173.6 7.0 %all-to-all-done = bf16[4,128,512]{2,1,0:T(8,128)(2,1)S(1)} async-done(((bf16[4,128,512]{2,1,0:T(8,128)(2,1)}), bf16[4,128,512]{2,1,0:T(8,128)(2,1)S(1)}, u32[]{:S(2)}, u32[]{:S(2)}) %all-to-all-start) | async-done | bytes 524320 | tf_op jit(solution)/shard_map/all_to_all | solution.py:390
  180.6 0.3 copy.28
  180.9 1.0 copy.29
  (1 shorter events, 0.0 us)
Async XLA Ops:
  158.5 6.8 %copy-start.1 = (s32[8,4]{0,1:T(4,128)S(1)}, s32[8,4]{0,1:T(4,128)}, u32[]{:S(2)}) copy-start(s32[8,4]{0,1:T(4,128)} %param.13) | copy-start | bytes 388
  158.5 7.1 %copy-start = (bf16[8,2,128,512]{3,2,1,0:T(8,128)(2,1)S(1)}, bf16[8,2,128,512]{3,2,1,0:T(8,128)(2,1)}, u32[]{:S(2)}) copy-start(bf16[8,2,128,512]{3,2,1,0:T(8,128)(2,1)} %get-tuple-element.12) | copy-start | bytes 6291460
  161.8 18.8 %all-to-all-start = ((bf16[4,128,512]{2,1,0:T(8,128)(2,1)}), bf16[4,128,512]{2,1,0:T(8,128)(2,1)S(1)}, u32[]{:S(2)}, u32[]{:S(2)}) async-start(bf16[4,128,512]{2,1,0:T(8,128)(2,1)} %fusion.3), calls=%async_computation | async-start | bytes 1048576 | tf_op jit(solution)/shard_map/all_to_all | solution.py:390
  165.6 1.4 copy-start.4
  167.0 2.2 %copy-start.3 = (bf16[32,32,768]{2,1,0:T(8,128)(2,1)S(1)}, bf16[32,32,768]{2,1,0:T(8,128)(2,1)}, u32[]{:S(2)}) copy-start(bf16[32,32,768]{2,1,0:T(8,128)(2,1)} %get-tuple-element.13) | copy-start | bytes 4718596
  169.2 2.2 %copy-start.2 = (bf16[32,32,768]{2,1,0:T(8,128)(2,1)S(1)}, bf16[32,32,768]{2,1,0:T(8,128)(2,1)}, u32[]{:S(2)}) copy-start(bf16[32,32,768]{2,1,0:T(8,128)(2,1)} %get-tuple-element.15) | copy-start | bytes 4718596
